TPU v7x, 512 devices: a whole 4x8x8 slice. The times are simulated.
512 devices in a mesh: pix: 16 (over z, core), frm: 32 (over y, x).
Axes of the slice: x: 4, y: 8, z: 8, core: 2. Of those that a mesh axis runs over, the one named last changes fastest.
Arguments:
- video: bfloat16 [16384, 8192], P('pix', 'frm'), may hold values from -6 to 6
- sparse: float32 [16384, 8192], P('pix', 'frm'), may hold values from -4 to 4
- multiplier: float32 [16384, 8192], P('pix', 'frm'), may hold values from -3 to 3
- start_block: bfloat16 [8192, 64], P('frm'), may hold values from -6 to 6
Outputs:
- sparse_next: float32 [16384, 8192], P('pix', 'frm')
- multiplier_next: float32 [16384, 8192], P('pix', 'frm')
- residual_ratio: float32 [8192], P('frm')
All inputs are finite; a program needn't handle non-finite values.
Results may differ from a plain program's by a relative error of at most 0.03.
Values may be sent and summed in bfloat16 or wider, within the bound.
No kernel may reach another device: no remote copies, remote signals or barrier semaphores. Data moves between devices by JAX's collectives and lax.ppermute only.
A program may use at most 64 MiB of HBM per device.

v0:
```python
import jax
import jax.numpy as jnp
from jax import lax
from jax.sharding import PartitionSpec as P

mu_value = 1.25
sparse_cut = 0.8
shrink_ratio = 0.25
epsilon_value = 1e-06


def column_gram(matrix):
    return lax.dot_general(
        matrix, matrix, (((0,), (0,)), ((), ())), precision=lax.Precision.HIGHEST
    )


def per_device(video, sparse, multiplier, start_block):
    highest = lax.Precision.HIGHEST
    video_full = video.astype(jnp.float32)
    working = (video_full - sparse + multiplier / mu_value).astype(jnp.bfloat16)
    partial_rows = jnp.dot(working, start_block, preferred_element_type=jnp.float32)
    across = lax.psum(partial_rows.astype(jnp.bfloat16), "frm")
    krylov_part = lax.dot_general(
        working, across, (((0,), (0,)), ((), ())), preferred_element_type=jnp.float32
    )
    krylov = lax.psum(krylov_part, "pix")
    gram_block = lax.psum(column_gram(krylov), "frm")
    factor = jnp.linalg.cholesky(gram_block)
    subspace = jax.scipy.linalg.solve_triangular(factor, krylov.T, lower=True).T
    subspace_half = subspace.astype(jnp.bfloat16)
    projected_part = jnp.dot(working, subspace_half, preferred_element_type=jnp.float32)
    projected = lax.psum(projected_part, "frm")
    projected_gram = lax.psum(column_gram(projected), "pix")
    block_width = projected_gram.shape[0]
    shrink_level = jnp.trace(projected_gram) * (shrink_ratio / block_width)
    shifted_gram = projected_gram + shrink_level * jnp.eye(block_width, dtype=jnp.float32)
    weights = jax.scipy.linalg.cho_solve((jnp.linalg.cholesky(shifted_gram), True), projected_gram)
    expanded = jnp.dot(subspace, weights.T, precision=highest)
    low_rank = jnp.dot(projected, expanded.T, precision=highest)
    shifted = video_full - low_rank + multiplier / mu_value
    sparse_next = jnp.sign(shifted) * jnp.maximum(jnp.abs(shifted) - sparse_cut, 0.0)
    residual = video_full - low_rank - sparse_next
    multiplier_next = multiplier + mu_value * residual
    residual_sq = jnp.sum(residual * residual, axis=0)
    video_sq = jnp.sum(video_full * video_full, axis=0)
    residual_sq, video_sq = lax.psum((residual_sq, video_sq), "pix")
    residual_ratio = jnp.sqrt(residual_sq / (video_sq + epsilon_value))
    return (sparse_next, multiplier_next, residual_ratio)


def solution(mesh):
    placed = (P("pix", "frm"), P("pix", "frm"), P("pix", "frm"), P("frm", None))
    return jax.shard_map(
        per_device,
        mesh=mesh,
        in_specs=placed,
        out_specs=(P("pix", "frm"), P("pix", "frm"), P("frm")),
        check_vma=False,
    )
```

profile of v0, /device:TPU:1, one launch (start us, length us, event | category | flops | bytes accessed | tf_op | source)
XLA Modules:
  0.0 680.5 jit_solution(18187934344375457308)
XLA Ops:
  7.2 1.9 fusion.2
  9.2 1.0 convolution_convert_fusion
  10.2 158.0 %all-reduce.5.cloned.1.call-done = bf16[1024,64]{1,0:T(8,128)(2,1)} async-done(((bf16[1024,64]{1,0:T(8,128)(2,1)}), bf16[1024,64]{1,0:T(8,128)(2,1)}) %all-reduce.5.cloned.1.call-update) | async-done | bytes 131088 | tf_op jit(solution)/shard_map/psum | solution.py:23
  168.2 1.8 fusion.20
  170.1 107.8 %all-reduce.7.cloned.1.call-done = f32[256,64]{0,1:T(8,128)} async-done(((f32[256,64]{0,1:T(8,128)}), f32[256,64]{0,1:T(8,128)}) %all-reduce.7.cloned.1.call-update) | async-done | bytes 65552 | tf_op jit(solution)/shard_map/psum | solution.py:27
  277.9 1.1 fusion.21
  279.1 115.4 %psum.51 = f32[64,64]{0,1:T(8,128)S(1)} all-reduce(f32[64,64]{0,1:T(8,128)S(1)} %fusion.21), channel_id=1, replica_groups=mesh['pix'=16,'frm'=32] {'frm'}, use_global_device_ids=true, to_apply=%region_2.0 | all-reduce | flops 4096 | bytes 32768 | tf_op jit(solution)/shard_map/psum | solution.py:28
  394.5 5.8 cholesky.44
  400.4 0.6 compare_reduce_fusion.1
  401.1 0.7 fusion.3
  401.7 4.9 custom-call.13
  406.9 1.0 fusion.17
  407.9 171.2 %all-reduce.9.cloned.1.call-done = f32[1024,64]{0,1:T(8,128)} async-done(((f32[1024,64]{0,1:T(8,128)}), f32[1024,64]{0,1:T(8,128)}) %all-reduce.9.cloned.1.call-update) | async-done | bytes 262160 | tf_op jit(solution)/shard_map/psum | solution.py:33
  579.1 1.4 fusion.22
  580.5 48.3 %psum.53 = f32[64,64]{1,0:T(8,128)S(1)} all-reduce(f32[64,64]{1,0:T(8,128)S(1)} %fusion.22), channel_id=1, replica_groups=mesh['pix'=16,'frm'=32] {'pix'}, use_global_device_ids=true, to_apply=%region_6.8 | all-reduce | flops 4096 | bytes 32768 | tf_op jit(solution)/shard_map/psum | solution.py:34
  628.8 0.6 fusion.15
  630.3 5.9 cholesky.55
  636.2 0.6 compare_reduce_fusion
  636.8 0.7 fusion.4
  637.5 4.9 custom-call.14
  643.2 2.6 multiply_reduce_fusion
  645.8 26.4 %all-reduce = (f32[256]{0:T(256)S(1)}, f32[256]{0:T(256)S(1)}) all-reduce(f32[256]{0:T(256)S(1)} %get-tuple-element.6, f32[256]{0:T(256)S(1)} %get-tuple-element.8), channel_id=1, replica_groups=mesh['pix'=16,'frm'=32] {'pix'}, use_global_device_ids=true, to_apply=%region_9.11 | all-reduce | flops 512 | bytes 4096 | tf_op jit(solution)/shard_map/psum | solution.py:47
  672.2 0.6 fusion.19
  672.8 1.2 multiply_add_fusion
  (28 shorter events, 1.6 us)
Async XLA Ops:
  7.2 2.0 copy-start
  7.2 161.0 %all-reduce.5.cloned.1.call-start = ((), (), s32[]{:S(2)}) async-start(), calls=%async_computation | async-start | bytes 524288 | tf_op jit(solution)/shard_map/psum | solution.py:23
  10.2 267.7 %all-reduce.7.cloned.1.call-start = ((), (), s32[]{:S(2)}) async-start(), calls=%async_computation.1 | async-start | bytes 131072 | tf_op jit(solution)/shard_map/psum | solution.py:27
  170.0 409.0 %all-reduce.9.cloned.1.call-start = ((), (), s32[]{:S(2)}) async-start(), calls=%async_computation.2 | async-start | bytes 524288 | tf_op jit(solution)/shard_map/psum | solution.py:33
  394.5 12.1 %copy-start.4 = (f32[256,64]{0,1:T(8,128)S(1)}, f32[256,64]{0,1:T(8,128)}, u32[]{:S(2)}) copy-start(f32[256,64]{0,1:T(8,128)} %all-reduce.7.cloned.1.call-done) | copy-start | bytes 196612
  407.9 235.3 %copy-start.1 = (f32[1024,256]{1,0:T(8,128)S(1)}, f32[1024,256]{1,0:T(8,128)}, u32[]{:S(2)}) copy-start(f32[1024,256]{1,0:T(8,128)} %param.7) | copy-start | bytes 3145732
  636.1 7.1 %copy-start.3 = (f32[1024,64]{0,1:T(8,128)S(1)}, f32[1024,64]{0,1:T(8,128)}, u32[]{:S(2)}) copy-start(f32[1024,64]{0,1:T(8,128)} %all-reduce.9.cloned.1.call-done) | copy-start | bytes 786436
  645.8 28.2 %copy-start.2 = (f32[1024,256]{1,0:T(8,128)}, f32[1024,256]{1,0:T(8,128)S(1)}, u32[]{:S(2)}) copy-start(f32[1024,256]{1,0:T(8,128)S(1)} %get-tuple-element.7) | copy-start | bytes 3145732
Sparse Core Ops, SparseCore 0:
  12.0 156.1 all-reduce.4
  171.1 106.8 all-reduce.6
  408.0 170.9 all-reduce.8
where the time goes:
time: 681 us
  waiting for transfers between devices  437 us (64%)
  blocking collectives  190 us (28%)
  other arithmetic  28.5 us (4%)
  between operations  14.6 us (2%)
  matrix products  9.93 us (1%)
    psum x1, waiting for transfers between devices, per_device(): projected = lax.psum(projected_part, 'frm')  171 us
    psum x1, waiting for transfers between devices, per_device(): across = lax.psum(partial_rows.astype(jnp.bfloat16), 'frm')  158 us
    psum x1, blocking collectives, per_device(): gram_block = lax.psum(column_gram(krylov), 'frm')  115 us
    psum x1, waiting for transfers between devices, per_device(): krylov = lax.psum(krylov_part, 'pix')  108 us
    psum x1, blocking collectives, per_device(): projected_gram = lax.psum(column_gram(projected), 'pix')  48.3 us
    psum x1, blocking collectives, per_device(): residual_sq, video_sq = lax.psum((residual_sq, video_sq), 'pix')  26.4 us
  transfers between devices with their start and end apart: 3, of which 3 were waited for; matrix products, arithmetic and copies ran while one was open for 0% of the time, Pallas kernels for 0%

commit v1 on v0

v1 whole, which is shorter than its diff:
```python
import functools

import jax
import jax.numpy as jnp
from jax import lax
from jax.experimental import pallas as pl
from jax.experimental.pallas import tpu as pltpu
from jax.sharding import PartitionSpec as P

mu_value = 1.25
inverse_mu = 0.8
sparse_cut = 0.8
shrink_ratio = 0.25
epsilon_value = 1e-06

f32 = jnp.float32
bf16 = jnp.bfloat16
highest = lax.Precision.HIGHEST

FRM = 32
PIX = 16
ROWS = 1024
HALF = 512
COLS = 256
RANK = 64
STEPS = 4
TILE = HALF // STEPS
SLICE = HALF // FRM

vmem = pl.BlockSpec(memory_space=pltpu.VMEM)
params = pltpu.CompilerParams(vmem_limit_bytes=40 * 1024 * 1024)


def dot_nt(a, b, **kw):
    return lax.dot_general(a, b, (((1,), (1,)), ((), ())), preferred_element_type=f32, **kw)


def dot_tn(a, b, **kw):
    return lax.dot_general(a, b, (((0,), (0,)), ((), ())), preferred_element_type=f32, **kw)


def dot_nn(a, b, **kw):
    return lax.dot_general(a, b, (((1,), (0,)), ((), ())), preferred_element_type=f32, **kw)


def split_two(x):
    hi = x.astype(bf16)
    return hi, (x - hi.astype(f32)).astype(bf16)


def split_three(x):
    hi = x.astype(bf16)
    rest = x - hi.astype(f32)
    mid = rest.astype(bf16)
    return hi, mid, (rest - mid.astype(f32)).astype(bf16)


def sub_iota():
    return lax.broadcasted_iota(jnp.int32, (8, 128), 0)


def lane_iota():
    return lax.broadcasted_iota(jnp.int32, (8, 128), 1)


def row_of(x, k):
    return jnp.broadcast_to(x[k : k + 1, :], (8, 128))


def column_of(x, c):
    return jnp.broadcast_to(x[:, c : c + 1], (8, 128))


def augment(a):
    blocks = []
    for b in range(8):
        eye = jnp.where(lane_iota() == sub_iota() + (8 * b + 64), 1.0, 0.0).astype(f32)
        part = a[8 * b : 8 * b + 8]
        blocks.append(jnp.where(lane_iota() < 64, jnp.concatenate([part, part], axis=1), eye))
    return blocks


def eliminate(blocks, factor):
    sub = sub_iota()
    rows = []
    for b in range(8):
        lead = blocks[b]
        cols = [column_of(lead, 8 * b + j) for j in range(8)]
        for k in range(8):
            at = sub == k
            pivot_row, pivot = row_of(lead, k), row_of(cols[k], k)
            if factor:
                root = lax.rsqrt(pivot)
                rows.append(pivot_row * root)
                inverse = root * root
            else:
                inverse = 1.0 / pivot
            scaled = pivot_row * inverse
            mult = cols[k]
            lead = jnp.where(at, scaled, lead - mult * scaled)
            for j in range(k + 1, 8):
                entry = row_of(cols[j], k) * inverse
                cols[j] = jnp.where(at, entry, cols[j] - mult * entry)
        blocks[b] = lead
        lead_rows = [row_of(lead, j) for j in range(8)]
        for i in range(b + 1 if factor else 0, 8):
            if i == b:
                continue
            block = blocks[i]
            total = block
            for j in range(8):
                total = total - column_of(block, 8 * b + j) * lead_rows[j]
            blocks[i] = total
    return rows if factor else blocks


def start_kernel(video, sparse, multiplier, start, working, across):
    start_block = start[...]
    halves = []
    for h in range(2):
        value = video[h].astype(f32) - sparse[h] + multiplier[h] * inverse_mu
        value = value.astype(bf16)
        working[h] = value
        halves.append(dot_nn(value, start_block))
    across[...] = jnp.concatenate(halves, axis=1).astype(bf16)


def sum_kernel(peers, x, out):
    total = x[0].astype(f32)
    for i in range(1, x.shape[0]):
        total = total + x[i].astype(f32)
    total = total.astype(out.dtype)
    for i in range(peers):
        out[i] = total


def krylov_kernel(across, working, out):
    packed = across[...].reshape(HALF, 128)
    first = dot_tn(packed, working[0])
    second = dot_tn(packed, working[1])
    krylov = first[:RANK] + second[RANK:]
    for i in range(8):
        out[i] = krylov[8 * i : 8 * i + 8, :128]
        out[8 + i] = krylov[8 * i : 8 * i + 8, 128:]


def project_kernel(gathered, working, krylov_out, out):
    packed = gathered[...].reshape(128, 128)
    krylov = jnp.concatenate([packed[:RANK], packed[RANK:]], axis=1)
    krylov_out[...] = krylov
    zero = jnp.zeros((RANK, COLS), bf16)
    total = None
    for part in reversed(split_three(krylov)):
        low = dot_nt(working[0], jnp.concatenate([part, zero], axis=0))
        high = dot_nt(working[1], jnp.concatenate([zero, part], axis=0))
        total = low + high if total is None else total + (low + high)
    gram = dot_nt(krylov, krylov, precision=highest)
    gram = jnp.concatenate([gram[:32], gram[32:]], axis=1)
    blank = jnp.zeros((7, 128), f32)
    for i in range(FRM):
        out[i, :SLICE] = total[SLICE * i : SLICE * i + SLICE]
        out[i, SLICE:] = jnp.concatenate([gram[i : i + 1], blank], axis=0)


def basis_kernel(gathered, krylov, projected_out, subspace_out, out, rows_ref):
    gram = jnp.concatenate([gathered[i, SLICE : SLICE + 1] for i in range(FRM)], axis=0)
    gram = jnp.concatenate([gram[:, :RANK], gram[:, RANK:]], axis=0)
    for i, row in enumerate(eliminate(augment(gram), True)):
        rows_ref[i : i + 1] = row[0:1]
    inverse = rows_ref[:, RANK:]
    zero = jnp.zeros((RANK, RANK), f32)
    pair = jnp.concatenate(
        [jnp.concatenate([inverse, zero], axis=1), jnp.concatenate([zero, inverse], axis=1)], axis=0
    )
    packed = gathered[:, :SLICE].reshape(HALF, 128)
    projected = dot_nt(packed, pair, precision=highest)
    projected_out[...] = projected
    subspace_out[...] = dot_nn(inverse, krylov[...], precision=highest)
    hi, lo = split_two(projected)
    gram = dot_tn(hi, hi) + (dot_tn(hi, lo) + dot_tn(lo, hi))
    gram = gram[:RANK, :RANK] + gram[RANK:, RANK:]
    gram = jnp.concatenate([gram[:32], gram[32:]], axis=1).astype(bf16)
    for i in range(PIX):
        out[i] = gram


def finish_kernel(grams, subspace, video, multiplier, projected, sparse_out, multiplier_out, out, weighted, sums):
    step = pl.program_id(0)

    @pl.when(step == 0)
    def _():
        gram = grams[0].astype(f32)
        for i in range(1, PIX):
            gram = gram + grams[i].astype(f32)
        gram = jnp.concatenate([gram[:, :RANK], gram[:, RANK:]], axis=0)
        rows = lax.broadcasted_iota(jnp.int32, (RANK, RANK), 0)
        cols = lax.broadcasted_iota(jnp.int32, (RANK, RANK), 1)
        eye = jnp.where(rows == cols, 1.0, 0.0).astype(f32)
        level = jnp.sum(jnp.sum(gram * eye, axis=0, keepdims=True), axis=1, keepdims=True) * (shrink_ratio / RANK)
        blocks = eliminate(augment(gram + level * eye), False)
        inverse = jnp.concatenate(blocks, axis=0)[:, RANK:]
        weights = eye - level * inverse
        mixed = dot_nn(weights, subspace[...], precision=highest)
        zero = jnp.zeros((RANK, COLS), bf16)
        for i, part in enumerate(split_two(mixed)):
            weighted[0, i] = jnp.concatenate([part, zero], axis=0)
            weighted[1, i] = jnp.concatenate([zero, part], axis=0)
        sums[...] = jnp.zeros_like(sums)

    hi, lo = split_two(projected[...])
    for h in range(2):
        low_rank = dot_nn(hi, weighted[h, 0]) + (dot_nn(hi, weighted[h, 1]) + dot_nn(lo, weighted[h, 0]))
        video_full = video[h].astype(f32)
        held = multiplier[h]
        base = video_full - low_rank
        shifted = base + held * inverse_mu
        sparse_next = shifted - jnp.clip(shifted, -sparse_cut, sparse_cut)
        residual = base - sparse_next
        sparse_out[h] = sparse_next
        multiplier_out[h] = held + mu_value * residual
        squares = (residual * residual).reshape(TILE // 8, 8, COLS)
        sums[0] += jnp.sum(squares, axis=0)
        squares = (video_full * video_full).reshape(TILE // 8, 8, COLS)
        sums[1] += jnp.sum(squares, axis=0)

    @pl.when(step == STEPS - 1)
    def _():
        residual_sq = jnp.sum(sums[0], axis=0, keepdims=True)
        video_sq = jnp.sum(sums[1], axis=0, keepdims=True)
        tile = jnp.concatenate(
            [residual_sq[:, :128], residual_sq[:, 128:], video_sq[:, :128], video_sq[:, 128:], jnp.zeros((4, 128), f32)],
            axis=0,
        )
        for i in range(PIX):
            out[i] = tile


def ratio_kernel(x, out):
    total = x[0]
    for i in range(1, PIX):
        total = total + x[i]
    out[...] = jnp.sqrt(total[0:2] / (total[2:4] + epsilon_value))


def struct(shape, dtype=f32):
    return jax.ShapeDtypeStruct(shape, dtype)


def whole(kernel, outs, count, **kw):
    return pl.pallas_call(
        kernel,
        out_shape=outs,
        in_specs=[vmem] * count,
        out_specs=jax.tree.map(lambda _: vmem, outs),
        compiler_params=params,
        **kw,
    )


def exchange(x, axis):
    return lax.all_to_all(x, axis, 0, 0)


def per_device(video, sparse, multiplier, start_block):
    video, sparse, multiplier = (x.reshape(2, HALF, COLS) for x in (video, sparse, multiplier))
    tall = pl.BlockSpec((2, TILE, COLS), lambda i: (0, i, 0))
    packed = pl.BlockSpec((TILE, 128), lambda i: (i, 0))

    working, across = pl.pallas_call(
        start_kernel,
        grid=(STEPS,),
        out_shape=(struct((2, HALF, COLS), bf16), struct((HALF, 128), bf16)),
        in_specs=[tall, tall, tall, pl.BlockSpec((COLS, RANK), lambda i: (0, 0))],
        out_specs=(tall, packed),
        compiler_params=params,
    )(video, sparse, multiplier, start_block)

    across = exchange(across.reshape(FRM, SLICE, 128), "frm")
    across = whole(functools.partial(sum_kernel, FRM), struct((FRM, SLICE, 128), bf16), 1)(across)
    across = exchange(across, "frm")

    krylov = whole(krylov_kernel, struct((PIX, 8, 128)), 2)(across, working)
    krylov = exchange(krylov, "pix")
    krylov = whole(functools.partial(sum_kernel, PIX), struct((PIX, 8, 128)), 1)(krylov)
    krylov = exchange(krylov, "pix")

    wide = struct((FRM, SLICE + 8, 128))
    krylov, projected = whole(project_kernel, (struct((RANK, COLS)), wide), 2)(krylov, working)
    projected = exchange(projected, "frm")
    projected = whole(functools.partial(sum_kernel, FRM), wide, 1)(projected)
    projected = exchange(projected, "frm")

    projected, subspace, grams = whole(
        basis_kernel,
        (struct((HALF, 128)), struct((RANK, COLS)), struct((PIX, 32, 128), bf16)),
        2,
        scratch_shapes=[pltpu.VMEM((RANK, 128), f32)],
    )(projected, krylov)
    grams = exchange(grams, "pix")

    sparse_next, multiplier_next, sums = pl.pallas_call(
        finish_kernel,
        grid=(STEPS,),
        out_shape=(struct((2, HALF, COLS)), struct((2, HALF, COLS)), struct((PIX, 8, 128))),
        in_specs=[
            pl.BlockSpec((PIX, 32, 128), lambda i: (0, 0, 0)),
            pl.BlockSpec((RANK, COLS), lambda i: (0, 0)),
            tall,
            tall,
            packed,
        ],
        out_specs=(tall, tall, pl.BlockSpec((PIX, 8, 128), lambda i: (0, 0, 0))),
        scratch_shapes=[pltpu.VMEM((2, 2, 128, COLS), bf16), pltpu.VMEM((2, 8, COLS), f32)],
        compiler_params=params,
    )(grams, subspace, video, multiplier, projected)
    sums = exchange(sums, "pix")
    ratio = whole(ratio_kernel, struct((2, 128)), 1)(sums)

    shape = (ROWS, COLS)
    return sparse_next.reshape(shape), multiplier_next.reshape(shape), ratio.reshape(COLS)


def solution(mesh):
    placed = (P("pix", "frm"), P("pix", "frm"), P("pix", "frm"), P("frm", None))
    return jax.shard_map(
        per_device,
        mesh=mesh,
        in_specs=placed,
        out_specs=(P("pix", "frm"), P("pix", "frm"), P("frm")),
        check_vma=False,
    )
```

time: 681 us -> 141 us (0.21)
  waiting for transfers between devices: 437 us -> 0 us
  blocking collectives: 190 us -> 124 us
  other arithmetic: 28.5 us -> 0 us
  between operations: 14.6 us -> 0.69 us
  Pallas kernels: 0 us -> 11.5 us
  matrix products: 9.93 us -> 0 us
    psum x3 -> x0, waiting for transfers between devices: 437 us -> none  [the longest x1 171 us: per_device(): projected = lax.psum(projected_part, 'frm')]
    psum x3 -> x0, blocking collectives: 190 us -> none  [the longest x1 115 us: per_device(): gram_block = lax.psum(column_gram(krylov), 'frm')]
    all_to_all x0 -> x8, blocking collectives: none -> 124 us  [exchange(): return lax.all_to_all(x, axis, 0, 0)]
    another operation x10 -> x0, other arithmetic: 24.1 us -> none  [the longest x3 6.52 us: per_device(): jnp.linalg.cholesky(shifted_gram)]
    pallas_call x0 -> x9, Pallas kernels: none -> 11.5 us  [the longest x1 5.47 us: per_device(): pl.pallas_call(finish_kernel, grid=(STEPS,), out_shape=(struct((2, HALF,...]
    dot_general x7 -> x0, matrix products: 9.26 us -> none  [the longest x1 2.57 us: per_device(): low_rank = jnp.dot(projected, expanded.T, precision=highest)]
  transfers between devices with their start and end apart: 3 -> 0, of which waited for: 3 -> 0; matrix products, arithmetic and copies ran while one was open for 0% -> 0% of each run, Pallas kernels for 0% -> 0%
where the time goes in v1:
time: 141 us; the launch traced here: 140 us
  blocking collectives  124 us (88%)
  Pallas kernels  11.5 us (8%)
  local copies, waits for them, and re-layouts  4.37 us (3%)
    all_to_all x8, blocking collectives, exchange(): return lax.all_to_all(x, axis, 0, 0)  124 us
    pallas_call x1, Pallas kernels, per_device(): pl.pallas_call(finish_kernel, grid=(STEPS,), out_shape=(struct((2, HALF,...  5.47 us
    unnamed x11, local copies, waits for them, and re-layouts  4.37 us
    pallas_call x1, Pallas kernels, per_device(): whole(basis_kernel, (struct((HALF, 128)), struct((RANK, COLS)), struct((P...  3.23 us

profile of v1, /device:TPU:1, one launch (start us, length us, event | category | flops | bytes accessed | tf_op | source)
XLA Modules:
  0.0 140.3 jit_solution(4894778879849757855)
XLA Ops:
  0.6 0.9 copy.7.start
  1.5 0.0 copy-start
  1.5 1.2 copy-done
  2.7 0.0 copy-start.2
  2.7 1.0 copy-done.2
  3.8 0.0 copy-start.4
  3.8 1.2 copy-done.4
  5.0 1.2 shard_map.67
  6.2 19.6 %all_to_all.40.x = bf16[32,16,128]{2,1,0:T(8,128)(2,1)S(1)} all-to-all(bf16[32,16,128]{2,1,0:T(8,128)(2,1)S(1)} %bitcast.12), channel_id=1, replica_groups=mesh['pix'=16,'frm'=32] {'frm'}, dimensions={0} | all-to-all | bytes 262144 | tf_op jit(solution)/shard_map/all_to_all | solution.py:261
  25.9 12.6 %all_to_all.41.across = bf16[32,16,128]{2,1,0:T(8,128)(2,1)S(1)} all-to-all(bf16[32,16,128]{2,1,0:T(8,128)(2,1)S(1)} %shard_map.68), channel_id=1, replica_groups=mesh['pix'=16,'frm'=32] {'frm'}, dimensions={0} | all-to-all | bytes 262144 | tf_op jit(solution)/shard_map/all_to_all | solution.py:261
  38.5 0.2 shard_map.69
  38.8 21.3 %all_to_all.42.x = f32[16,8,128]{2,1,0:T(8,128)S(1)} all-to-all(f32[16,8,128]{2,1,0:T(8,128)S(1)} %shard_map.69), channel_id=1, replica_groups=mesh['pix'=16,'frm'=32] {'pix'}, dimensions={0} | all-to-all | bytes 131072 | tf_op jit(solution)/shard_map/all_to_all | solution.py:261
  60.1 10.4 %all_to_all.43.gathered = f32[16,8,128]{2,1,0:T(8,128)S(1)} all-to-all(f32[16,8,128]{2,1,0:T(8,128)S(1)} %shard_map.70), channel_id=1, replica_groups=mesh['pix'=16,'frm'=32] {'pix'}, dimensions={0} | all-to-all | bytes 131072 | tf_op jit(solution)/shard_map/all_to_all | solution.py:261
  70.5 0.7 shard_map.71
  71.2 17.5 %all_to_all.44.x = f32[32,24,128]{2,1,0:T(8,128)S(1)} all-to-all(f32[32,24,128]{2,1,0:T(8,128)S(1)} %get-tuple-element.15), channel_id=1, replica_groups=mesh['pix'=16,'frm'=32] {'frm'}, dimensions={0} | all-to-all | bytes 786432 | tf_op jit(solution)/shard_map/all_to_all | solution.py:261
  88.6 0.1 shard_map.72
  88.7 17.1 %all_to_all.45.gathered = f32[32,24,128]{2,1,0:T(8,128)S(1)} all-to-all(f32[32,24,128]{2,1,0:T(8,128)S(1)} %shard_map.72), channel_id=1, replica_groups=mesh['pix'=16,'frm'=32] {'frm'}, dimensions={0} | all-to-all | bytes 786432 | tf_op jit(solution)/shard_map/all_to_all | solution.py:261
  105.8 3.2 %shard_map.73 = (f32[512,128]{1,0:T(8,128)S(1)}, f32[64,256]{1,0:T(8,128)S(1)}, bf16[16,32,128]{2,1,0:T(8,128)(2,1)S(1)}) custom-call(f32[32,24,128]{2,1,0:T(8,128)S(1)} %all_to_all.45.gathered, f32[64,256]{1,0:T(8,128)S(1)} %get-tuple-element.16.krylov), custom_call_target="tpu_custom_call" | custom-call | tf_op jit(solution)/shard_map/pallas_call | solution.py:293
  109.1 15.0 %all_to_all.46.grams = bf16[16,32,128]{2,1,0:T(8,128)(2,1)S(1)} all-to-all(bf16[16,32,128]{2,1,0:T(8,128)(2,1)S(1)} %get-tuple-element.17), channel_id=1, replica_groups=mesh['pix'=16,'frm'=32] {'pix'}, dimensions={0} | all-to-all | bytes 262144 | tf_op jit(solution)/shard_map/all_to_all | solution.py:261
  124.0 0.0 copy-done.1
  124.0 0.0 copy-done.3
  124.0 5.5 %shard_map.74 = (f32[2,512,256]{2,1,0:T(8,128)}, f32[2,512,256]{2,1,0:T(8,128)}, f32[16,8,128]{2,1,0:T(8,128)S(1)}) custom-call(bf16[16,32,128]{2,1,0:T(8,128)(2,1)S(1)} %all_to_all.46.grams, f32[64,256]{1,0:T(8,128)S(1)} %get-tuple-element.18.subspace, bf16[2,512,256]{2,1,0:T(8,128)(2,1)S(1)} %bitcast.10, f32[2,512,256]{2,1,0:T(8,128)S(1)} %bitcast.8, ...), custom_call_target="tpu_custom_call" | custom-call | tf_op jit(solution)/shard_map/pallas_call | solution.py:301
  129.5 10.2 %all_to_all.47.x = f32[16,8,128]{2,1,0:T(8,128)S(1)} all-to-all(f32[16,8,128]{2,1,0:T(8,128)S(1)} %get-tuple-element.22), channel_id=1, replica_groups=mesh['pix'=16,'frm'=32] {'pix'}, dimensions={0} | all-to-all | bytes 131072 | tf_op jit(solution)/shard_map/all_to_all | solution.py:261
  139.7 0.6 shard_map.75
  (4 shorter events, 0.1 us)
Async XLA Ops:
  1.5 1.2 copy-start
  2.7 1.0 copy-start.2
  3.8 1.2 copy-start.4
  88.6 35.4 %copy-start.1 = (f32[1024,256]{1,0:T(8,128)S(1)}, f32[1024,256]{1,0:T(8,128)}, u32[]{:S(2)}) copy-start(f32[1024,256]{1,0:T(8,128)} %param.6) | copy-start | bytes 3145732
  105.8 18.2 %copy-start.3 = (bf16[1024,256]{1,0:T(8,128)(2,1)S(1)}, bf16[1024,256]{1,0:T(8,128)(2,1)}, u32[]{:S(2)}) copy-start(bf16[1024,256]{1,0:T(8,128)(2,1)} %param.4) | copy-start | bytes 1572868

commit v2 on v1

v2 whole, which is shorter than its diff:
```python
import functools

import jax
import jax.numpy as jnp
from jax import lax
from jax.experimental import pallas as pl
from jax.experimental.pallas import tpu as pltpu
from jax.sharding import PartitionSpec as P

mu_value = 1.25
inverse_mu = 0.8
sparse_cut = 0.8
shrink_ratio = 0.25
epsilon_value = 1e-06

f32 = jnp.float32
bf16 = jnp.bfloat16
highest = lax.Precision.HIGHEST

FRM = 32
PIX = 16
ROWS = 1024
HALF = 512
COLS = 256
RANK = 64
START_STEPS = 2
START_TILE = HALF // START_STEPS
STEPS = 4
TILE = HALF // STEPS
SLICE = HALF // FRM
CHUNK = SLICE + 1

vmem = pl.BlockSpec(memory_space=pltpu.VMEM)
params = pltpu.CompilerParams(vmem_limit_bytes=40 * 1024 * 1024)


def dot_nt(a, b, **kw):
    return lax.dot_general(a, b, (((1,), (1,)), ((), ())), preferred_element_type=f32, **kw)


def dot_tn(a, b, **kw):
    return lax.dot_general(a, b, (((0,), (0,)), ((), ())), preferred_element_type=f32, **kw)


def dot_nn(a, b, **kw):
    return lax.dot_general(a, b, (((1,), (0,)), ((), ())), preferred_element_type=f32, **kw)


def split_two(x):
    hi = x.astype(bf16)
    return hi, (x - hi.astype(f32)).astype(bf16)


def split_three(x):
    hi = x.astype(bf16)
    rest = x - hi.astype(f32)
    mid = rest.astype(bf16)
    return hi, mid, (rest - mid.astype(f32)).astype(bf16)


def sub_iota():
    return lax.broadcasted_iota(jnp.int32, (8, 128), 0)


def lane_iota():
    return lax.broadcasted_iota(jnp.int32, (8, 128), 1)


def row_of(x, k):
    return jnp.broadcast_to(x[k : k + 1, :], (8, 128))


def column_of(x, c):
    return jnp.broadcast_to(x[:, c : c + 1], (8, 128))


def augment(a):
    blocks = []
    for b in range(8):
        eye = jnp.where(lane_iota() == sub_iota() + (8 * b + 64), 1.0, 0.0).astype(f32)
        part = a[8 * b : 8 * b + 8]
        blocks.append(jnp.where(lane_iota() < 64, jnp.concatenate([part, part], axis=1), eye))
    return blocks


def eliminate(blocks, factor):
    sub = sub_iota()
    rows = []
    for b in range(8):
        lead = blocks[b]
        cols = [column_of(lead, 8 * b + j) for j in range(8)]
        for k in range(8):
            at = sub == k
            pivot_row, pivot = row_of(lead, k), row_of(cols[k], k)
            if factor:
                root = lax.rsqrt(pivot)
                rows.append(pivot_row * root)
                inverse = root * root
            else:
                inverse = 1.0 / pivot
            scaled = pivot_row * inverse
            mult = cols[k]
            lead = jnp.where(at, scaled, lead - mult * scaled)
            for j in range(k + 1, 8):
                entry = row_of(cols[j], k) * inverse
                cols[j] = jnp.where(at, entry, cols[j] - mult * entry)
        blocks[b] = lead
        lead_rows = [row_of(lead, j) for j in range(8)]
        for i in range(b + 1 if factor else 0, 8):
            if i == b:
                continue
            block = blocks[i]
            total = block
            for j in range(8):
                total = total - column_of(block, 8 * b + j) * lead_rows[j]
            blocks[i] = total
    return rows if factor else blocks


def start_kernel(video, sparse, multiplier, start, working, across, video_in, sparse_in, multiplier_in, start_in, sems):
    sources = ((video, video_in), (sparse, sparse_in), (multiplier, multiplier_in))
    copies = [pltpu.make_async_copy(start, start_in, sems.at[3 * START_STEPS])]
    for i in range(START_STEPS):
        rows = pl.ds(START_TILE * i, START_TILE)
        for j, (source, target) in enumerate(sources):
            copies.append(pltpu.make_async_copy(source.at[:, rows], target.at[:, rows], sems.at[3 * i + j]))
    for copy in copies:
        copy.start()
    copies[0].wait()
    for i in range(START_STEPS):
        rows = slice(START_TILE * i, START_TILE * i + START_TILE)
        for copy in copies[1 + 3 * i : 4 + 3 * i]:
            copy.wait()
        halves = []
        for h in range(2):
            value = video_in[h, rows].astype(f32) - sparse_in[h, rows] + multiplier_in[h, rows] * inverse_mu
            value = value.astype(bf16)
            working[h, rows] = value
            halves.append(dot_nt(value, start_in[...]))
        across[rows] = jnp.concatenate(halves, axis=1).astype(bf16)


def sum_kernel(peers, x, out):
    rows = x.shape[0] // peers
    total = x[:rows].astype(f32)
    for i in range(1, peers):
        total = total + x[rows * i : rows * i + rows].astype(f32)
    total = total.astype(out.dtype)
    for i in range(peers):
        out[rows * i : rows * i + rows] = total


def krylov_kernel(across, working, out):
    packed = across[...]
    first = dot_tn(packed, working[0])
    second = dot_tn(packed, working[1])
    krylov = first[:RANK] + second[RANK:]
    for i in range(8):
        out[8 * i : 8 * i + 8] = krylov[8 * i : 8 * i + 8, :128]
        out[RANK + 8 * i : RANK + 8 * i + 8] = krylov[8 * i : 8 * i + 8, 128:]


def project_kernel(gathered, working, krylov_out, out):
    packed = gathered[...]
    krylov = jnp.concatenate([packed[:RANK], packed[RANK:]], axis=1)
    krylov_out[...] = krylov
    zero = jnp.zeros((RANK, COLS), bf16)
    total = None
    for part in reversed(split_three(krylov)):
        low = dot_nt(working[0], jnp.concatenate([part, zero], axis=0))
        high = dot_nt(working[1], jnp.concatenate([zero, part], axis=0))
        total = low + high if total is None else total + (low + high)
    gram = dot_nt(krylov, krylov, precision=highest)
    gram = jnp.concatenate([gram[:32], gram[32:]], axis=1)
    for i in range(FRM):
        at = CHUNK * i
        out[at : at + SLICE] = total[SLICE * i : SLICE * i + SLICE]
        out[at + SLICE : at + CHUNK] = gram[i : i + 1]


def basis_kernel(gathered, krylov, projected_out, subspace_out, out, rows_ref):
    gram = jnp.concatenate([gathered[CHUNK * i + SLICE : CHUNK * i + CHUNK] for i in range(FRM)], axis=0)
    gram = jnp.concatenate([gram[:, :RANK], gram[:, RANK:]], axis=0)
    for i, row in enumerate(eliminate(augment(gram), True)):
        rows_ref[i : i + 1] = row[0:1]
    inverse = rows_ref[:, RANK:]
    zero = jnp.zeros((RANK, RANK), f32)
    pair = jnp.concatenate(
        [jnp.concatenate([inverse, zero], axis=1), jnp.concatenate([zero, inverse], axis=1)], axis=0
    )
    packed = jnp.concatenate([gathered[CHUNK * i : CHUNK * i + SLICE] for i in range(FRM)], axis=0)
    projected = dot_nt(packed, pair, precision=highest)
    projected_out[...] = projected
    subspace_out[...] = dot_nn(inverse, krylov[...], precision=highest)
    hi, lo = split_two(projected)
    gram = dot_tn(hi, hi) + (dot_tn(hi, lo) + dot_tn(lo, hi))
    gram = gram[:RANK, :RANK] + gram[RANK:, RANK:]
    gram = jnp.concatenate([gram[:32], gram[32:]], axis=1).astype(bf16)
    for i in range(PIX):
        out[32 * i : 32 * i + 32] = gram


def finish_kernel(grams, subspace, video, multiplier, projected, sparse_out, multiplier_out, out, near, sems):
    gram = grams[:32].astype(f32)
    for i in range(1, PIX):
        gram = gram + grams[32 * i : 32 * i + 32].astype(f32)
    gram = jnp.concatenate([gram[:, :RANK], gram[:, RANK:]], axis=0)
    rows = lax.broadcasted_iota(jnp.int32, (RANK, RANK), 0)
    cols = lax.broadcasted_iota(jnp.int32, (RANK, RANK), 1)
    eye = jnp.where(rows == cols, 1.0, 0.0).astype(f32)
    level = jnp.sum(jnp.sum(gram * eye, axis=0, keepdims=True), axis=1, keepdims=True) * (shrink_ratio / RANK)
    blocks = eliminate(augment(gram + level * eye), False)
    inverse = jnp.concatenate(blocks, axis=0)[:, RANK:]
    weights = eye - level * inverse
    mixed = dot_nn(weights, subspace[...], precision=highest)
    zero = jnp.zeros((RANK, COLS), bf16)
    parts = split_two(mixed)
    weighted = [[jnp.concatenate(pair, axis=0) for pair in ((part, zero), (zero, part))] for part in parts]

    residual_sq = jnp.zeros((8, COLS), f32)
    video_sq = jnp.zeros((8, COLS), f32)
    copies = []
    for i in range(STEPS):
        rows = slice(TILE * i, TILE * i + TILE)
        hi, lo = split_two(projected[rows])
        for h in range(2):
            low_rank = dot_nn(hi, weighted[0][h]) + (dot_nn(hi, weighted[1][h]) + dot_nn(lo, weighted[0][h]))
            video_full = video[h, rows].astype(f32)
            held = multiplier[h, rows]
            base = video_full - low_rank
            shifted = base + held * inverse_mu
            sparse_next = shifted - jnp.clip(shifted, -sparse_cut, sparse_cut)
            residual = base - sparse_next
            near[0, h, rows] = sparse_next
            near[1, h, rows] = held + mu_value * residual
            for j, target in enumerate((sparse_out, multiplier_out)):
                at = (h, pl.ds(TILE * i, TILE))
                copies.append(pltpu.make_async_copy(near.at[j].at[at], target.at[at], sems.at[len(copies)]))
                copies[-1].start()
            residual_sq += jnp.sum((residual * residual).reshape(TILE // 8, 8, COLS), axis=0)
            video_sq += jnp.sum((video_full * video_full).reshape(TILE // 8, 8, COLS), axis=0)
    residual_sq = jnp.sum(residual_sq, axis=0, keepdims=True)
    video_sq = jnp.sum(video_sq, axis=0, keepdims=True)
    tile = jnp.concatenate(
        [residual_sq[:, :128], residual_sq[:, 128:], video_sq[:, :128], video_sq[:, 128:], jnp.zeros((4, 128), f32)],
        axis=0,
    )
    for i in range(PIX):
        out[8 * i : 8 * i + 8] = tile
    for copy in copies:
        copy.wait()


def ratio_kernel(x, out):
    total = x[:8]
    for i in range(1, PIX):
        total = total + x[8 * i : 8 * i + 8]
    out[...] = jnp.sqrt(total[0:2] / (total[2:4] + epsilon_value))


def struct(shape, dtype=f32):
    return jax.ShapeDtypeStruct(shape, dtype)


def whole(kernel, outs, count, **kw):
    return pl.pallas_call(
        kernel,
        out_shape=outs,
        in_specs=[vmem] * count,
        out_specs=jax.tree.map(lambda _: vmem, outs),
        compiler_params=params,
        **kw,
    )


def exchange(x, axis):
    peers = FRM if axis == "frm" else PIX
    parts = (peers, 1, -1) if x.dtype == f32 else (peers, -1, 128)
    return lax.all_to_all(x.reshape(parts), axis, 0, 0).reshape(x.shape)


def per_device(video, sparse, multiplier, start_block):
    video, sparse, multiplier = (x.reshape(2, HALF, COLS) for x in (video, sparse, multiplier))
    far = pl.BlockSpec(memory_space=pltpu.HBM)
    working, across = pl.pallas_call(
        start_kernel,
        out_shape=(struct((2, HALF, COLS), bf16), struct((HALF, 128), bf16)),
        in_specs=[far] * 4,
        out_specs=(vmem, vmem),
        scratch_shapes=[
            pltpu.VMEM((2, HALF, COLS), bf16),
            pltpu.VMEM((2, HALF, COLS), f32),
            pltpu.VMEM((2, HALF, COLS), f32),
            pltpu.VMEM((RANK, COLS), bf16),
            pltpu.SemaphoreType.DMA((3 * START_STEPS + 1,)),
        ],
        compiler_params=params,
    )(*(pltpu.with_memory_space_constraint(x, pltpu.HBM) for x in (video, sparse, multiplier, start_block.T)))

    across = exchange(across, "frm")
    across = whole(functools.partial(sum_kernel, FRM), struct((HALF, 128), bf16), 1)(across)
    across = exchange(across, "frm")

    krylov = whole(krylov_kernel, struct((128, 128)), 2)(across, working)
    krylov = exchange(krylov, "pix")
    krylov = whole(functools.partial(sum_kernel, PIX), struct((128, 128)), 1)(krylov)
    krylov = exchange(krylov, "pix")

    wide = struct((FRM * CHUNK, 128))
    krylov, projected = whole(project_kernel, (struct((RANK, COLS)), wide), 2)(krylov, working)
    projected = exchange(projected, "frm")
    projected = whole(functools.partial(sum_kernel, FRM), wide, 1)(projected)
    projected = exchange(projected, "frm")

    projected, subspace, grams = whole(
        basis_kernel,
        (struct((HALF, 128)), struct((RANK, COLS)), struct((PIX * 32, 128), bf16)),
        2,
        scratch_shapes=[pltpu.VMEM((RANK, 128), f32)],
    )(projected, krylov)
    grams = exchange(grams, "pix")

    sparse_next, multiplier_next, sums = pl.pallas_call(
        finish_kernel,
        out_shape=(struct((2, HALF, COLS)), struct((2, HALF, COLS)), struct((PIX * 8, 128))),
        in_specs=[vmem] * 5,
        out_specs=(far, far, vmem),
        scratch_shapes=[pltpu.VMEM((2, 2, HALF, COLS), f32), pltpu.SemaphoreType.DMA((4 * STEPS,))],
        compiler_params=params,
    )(grams, subspace, video, multiplier, projected)
    sums = exchange(sums, "pix")
    ratio = whole(ratio_kernel, struct((2, 128)), 1)(sums)

    shape = (ROWS, COLS)
    return sparse_next.reshape(shape), multiplier_next.reshape(shape), ratio.reshape(COLS)


def solution(mesh):
    placed = (P("pix", "frm"), P("pix", "frm"), P("pix", "frm"), P("frm", None))
    return jax.shard_map(
        per_device,
        mesh=mesh,
        in_specs=placed,
        out_specs=(P("pix", "frm"), P("pix", "frm"), P("frm")),
        check_vma=False,
    )
```

time: 141 us -> 132 us (0.936)
  local copies, waits for them, and re-layouts: 4.37 us -> 0.01 us
  blocking collectives: 124 us -> 120 us
    unnamed x11 -> x4, local copies, waits for them, and re-layouts: 4.37 us -> 0.01 us
    all_to_all x8, blocking collectives: 124 us -> 120 us  [exchange(): return lax.all_to_all(x.reshape(parts), axis, 0, 0).reshape(x.shape)]
where the time goes in v2:
time: 132 us
  blocking collectives  120 us (91%)
  Pallas kernels  11.6 us (9%)
    all_to_all x8, blocking collectives, exchange(): return lax.all_to_all(x.reshape(parts), axis, 0, 0).reshape(x.shape)  120 us
    pallas_call x1, Pallas kernels, per_device(): pl.pallas_call(finish_kernel, out_shape=(struct((2, HALF, COLS)), struct(...  4.65 us
    pallas_call x1, Pallas kernels, per_device(): whole(basis_kernel, (struct((HALF, 128)), struct((RANK, COLS)), struct((P...  3.23 us

profile of v2, /device:TPU:1, one launch (start us, length us, event | category | flops | bytes accessed | tf_op | source)
XLA Modules:
  0.0 131.8 jit_solution(7539821636637066267)
XLA Ops:
  0.6 2.0 %shard_map.67 = (bf16[2,512,256]{2,1,0:T(8,128)(2,1)S(1)}, bf16[512,128]{1,0:T(8,128)(2,1)S(1)}) custom-call(bf16[2,512,256]{2,1,0:T(8,128)(2,1)} %bitcast.25, f32[2,512,256]{2,1,0:T(8,128)} %bitcast.43, f32[2,512,256]{2,1,0:T(8,128)} %bitcast.23, bf16[64,256]{1,0:T(8,128)(2,1)} %bitcast.44), custom_call_target="tpu_custom_call" | custom-call | tf_op jit(solution)/shard_map/pallas_call | solution.py:285
  2.7 19.6 %all_to_all.40 = bf16[32,16,128]{2,1,0:T(8,128)(2,1)S(1)} all-to-all(bf16[32,16,128]{2,1,0:T(8,128)(2,1)S(1)} %bitcast.41), channel_id=1, replica_groups=mesh['pix'=16,'frm'=32] {'frm'}, dimensions={0} | all-to-all | bytes 262144 | tf_op jit(solution)/shard_map/all_to_all | solution.py:279
  22.4 12.6 %all_to_all.41 = bf16[32,16,128]{2,1,0:T(8,128)(2,1)S(1)} all-to-all(bf16[32,16,128]{2,1,0:T(8,128)(2,1)S(1)} %bitcast.32), channel_id=1, replica_groups=mesh['pix'=16,'frm'=32] {'frm'}, dimensions={0} | all-to-all | bytes 262144 | tf_op jit(solution)/shard_map/all_to_all | solution.py:279
  35.0 0.2 shard_map.69
  35.3 21.3 %all_to_all.42 = f32[16,1,1024]{2,1,0:T(1,128)S(1)} all-to-all(f32[16,1,1024]{2,1,0:T(1,128)S(1)} %bitcast.39), channel_id=1, replica_groups=mesh['pix'=16,'frm'=32] {'pix'}, dimensions={0} | all-to-all | bytes 131072 | tf_op jit(solution)/shard_map/all_to_all | solution.py:279
  56.5 10.4 %all_to_all.43 = f32[16,1,1024]{2,1,0:T(1,128)S(1)} all-to-all(f32[16,1,1024]{2,1,0:T(1,128)S(1)} %bitcast.37), channel_id=1, replica_groups=mesh['pix'=16,'frm'=32] {'pix'}, dimensions={0} | all-to-all | bytes 131072 | tf_op jit(solution)/shard_map/all_to_all | solution.py:279
  66.9 0.7 shard_map.71
  67.6 0.0 copy-start
  67.6 15.2 %all_to_all.44 = f32[32,1,2176]{2,1,0:T(1,128)S(1)} all-to-all(f32[32,1,2176]{2,1,0:T(1,128)S(1)} %bitcast.34), channel_id=1, replica_groups=mesh['pix'=16,'frm'=32] {'frm'}, dimensions={0} | all-to-all | bytes 557056 | tf_op jit(solution)/shard_map/all_to_all | solution.py:279
  82.9 0.1 shard_map.72
  82.9 0.0 copy-start.1
  82.9 15.0 %all_to_all.45 = f32[32,1,2176]{2,1,0:T(1,128)S(1)} all-to-all(f32[32,1,2176]{2,1,0:T(1,128)S(1)} %bitcast.29), channel_id=1, replica_groups=mesh['pix'=16,'frm'=32] {'frm'}, dimensions={0} | all-to-all | bytes 557056 | tf_op jit(solution)/shard_map/all_to_all | solution.py:279
  98.0 3.2 %shard_map.73 = (f32[512,128]{1,0:T(8,128)S(1)}, f32[64,256]{1,0:T(8,128)S(1)}, bf16[512,128]{1,0:T(8,128)(2,1)S(1)}) custom-call(f32[544,128]{1,0:T(8,128)S(1)} %bitcast.27, f32[64,256]{1,0:T(8,128)S(1)} %get-tuple-element.16.krylov), custom_call_target="tpu_custom_call" | custom-call | tf_op jit(solution)/shard_map/pallas_call | solution.py:315
  101.2 15.1 %all_to_all.46 = bf16[16,32,128]{2,1,0:T(8,128)(2,1)S(1)} all-to-all(bf16[16,32,128]{2,1,0:T(8,128)(2,1)S(1)} %bitcast.40), channel_id=1, replica_groups=mesh['pix'=16,'frm'=32] {'pix'}, dimensions={0} | all-to-all | bytes 262144 | tf_op jit(solution)/shard_map/all_to_all | solution.py:279
  116.3 0.0 copy-done
  116.3 0.0 copy-done.1
  116.3 4.7 %shard_map.74 = (f32[2,512,256]{2,1,0:T(8,128)}, f32[2,512,256]{2,1,0:T(8,128)}, f32[128,128]{1,0:T(8,128)S(1)}) custom-call(bf16[512,128]{1,0:T(8,128)(2,1)S(1)} %bitcast.30, f32[64,256]{1,0:T(8,128)S(1)} %get-tuple-element.18.subspace, bf16[2,512,256]{2,1,0:T(8,128)(2,1)S(1)} %bitcast.26, f32[2,512,256]{2,1,0:T(8,128)S(1)} %bitcast.24, ...), custom_call_target="tpu_custom_call" | custom-call | tf_op jit(solution)/shard_map/pallas_call | solution.py:323
  121.0 10.2 %all_to_all.47 = f32[16,1,1024]{2,1,0:T(1,128)S(1)} all-to-all(f32[16,1,1024]{2,1,0:T(1,128)S(1)} %bitcast.42), channel_id=1, replica_groups=mesh['pix'=16,'frm'=32] {'pix'}, dimensions={0} | all-to-all | bytes 131072 | tf_op jit(solution)/shard_map/all_to_all | solution.py:279
  131.2 0.6 shard_map.75
  (2 shorter events, 0.1 us)
Async XLA Ops:
  67.6 48.7 %copy-start = (f32[1024,256]{1,0:T(8,128)S(1)}, f32[1024,256]{1,0:T(8,128)}, u32[]{:S(2)}) copy-start(f32[1024,256]{1,0:T(8,128)} %param.6) | copy-start | bytes 3145732
  82.9 33.4 %copy-start.1 = (bf16[1024,256]{1,0:T(8,128)(2,1)S(1)}, bf16[1024,256]{1,0:T(8,128)(2,1)}, u32[]{:S(2)}) copy-start(bf16[1024,256]{1,0:T(8,128)(2,1)} %param.4) | copy-start | bytes 1572868

commit v3 on v2

--- a/solution.py
+++ b/solution.py
@@ -83,38 +83,68 @@
     return blocks
 
 
-def eliminate(blocks, factor):
+def fold(block, cols, rows):
+    terms = [col * row for col, row in zip(cols, rows)]
+    while len(terms) > 1:
+        terms = [x + y for x, y in zip(terms[::2], terms[1::2])]
+    return block - terms[0]
+
+
+def rows_of(x):
+    return [row_of(x, j) for j in range(8)]
+
+
+def invert(blocks):
+    blocks = list(blocks)
     sub = sub_iota()
-    rows = []
     for b in range(8):
         lead = blocks[b]
         cols = [column_of(lead, 8 * b + j) for j in range(8)]
+        others = [i % 8 for i in range(b + 1, b + 8)]
+        mults = {i: [column_of(blocks[i], 8 * b + j) for j in range(8)] for i in others}
         for k in range(8):
-            at = sub == k
-            pivot_row, pivot = row_of(lead, k), row_of(cols[k], k)
-            if factor:
-                root = lax.rsqrt(pivot)
-                rows.append(pivot_row * root)
-                inverse = root * root
-            else:
-                inverse = 1.0 / pivot
-            scaled = pivot_row * inverse
-            mult = cols[k]
-            lead = jnp.where(at, scaled, lead - mult * scaled)
+            inverse = 1.0 / row_of(cols[k], k)
+            mult = cols[k] * inverse
             for j in range(k + 1, 8):
-                entry = row_of(cols[j], k) * inverse
-                cols[j] = jnp.where(at, entry, cols[j] - mult * entry)
+                row = row_of(cols[j], k)
+                cols[j] = jnp.where(sub == k, row * inverse, cols[j] - mult * row)
+            row = row_of(lead, k)
+            lead = jnp.where(sub == k, row * inverse, lead - mult * row)
         blocks[b] = lead
-        lead_rows = [row_of(lead, j) for j in range(8)]
-        for i in range(b + 1 if factor else 0, 8):
-            if i == b:
-                continue
-            block = blocks[i]
-            total = block
-            for j in range(8):
-                total = total - column_of(block, 8 * b + j) * lead_rows[j]
-            blocks[i] = total
-    return rows if factor else blocks
+        lead_rows = rows_of(lead)
+        for i in others:
+            blocks[i] = fold(blocks[i], mults[i], lead_rows)
+    return blocks
+
+
+def factorize(blocks):
+    blocks = [list(block) for block in blocks]
+    sub = sub_iota()
+    rows = []
+    cols = [column_of(blocks[0][0], j) for j in range(8)]
+    for b in range(8):
+        lead, last = blocks[b], b == 7
+        mults = {i: [column_of(blocks[i][0], 8 * b + j) for j in range(8)] for i in range(b + 1, 8)}
+        if not last:
+            ahead = [column_of(blocks[b + 1][0], 8 * b + 8 + j) for j in range(8)]
+            cols = cols + [column_of(lead[0], 8 * b + 8 + j) for j in range(8)]
+        for k in range(8):
+            lead_row = [row_of(x, k) for x in lead]
+            root = lax.rsqrt(row_of(cols[k], k))
+            rows.append([x * root for x in lead_row])
+            inverse = root * root
+            mult = cols[k] * inverse
+            for j in range(k + 1, len(cols)):
+                row = row_of(cols[j], k)
+                cols[j] = jnp.where(sub == k, row * inverse, cols[j] - mult * row)
+            lead = [jnp.where(sub == k, y * inverse, x - mult * y) for x, y in zip(lead, lead_row)]
+        if last:
+            break
+        cols = [fold(ahead[j], mults[b + 1], rows_of(cols[8 + j])) for j in range(8)]
+        lead_rows = [rows_of(x) for x in lead]
+        for i in range(b + 1, 8):
+            blocks[i] = [fold(x, mults[i], y) for x, y in zip(blocks[i], lead_rows)]
+    return rows
 
 
 def start_kernel(video, sparse, multiplier, start, working, across, video_in, sparse_in, multiplier_in, start_in, sems):
@@ -165,11 +195,12 @@
     krylov = jnp.concatenate([packed[:RANK], packed[RANK:]], axis=1)
     krylov_out[...] = krylov
     zero = jnp.zeros((RANK, COLS), bf16)
-    total = None
-    for part in reversed(split_three(krylov)):
-        low = dot_nt(working[0], jnp.concatenate([part, zero], axis=0))
-        high = dot_nt(working[1], jnp.concatenate([zero, part], axis=0))
-        total = low + high if total is None else total + (low + high)
+    first, second, third = split_three(krylov)
+    low = dot_nt(working[0], jnp.concatenate([first, zero, second, zero], axis=0))
+    high = dot_nt(working[1], jnp.concatenate([zero, first, zero, second], axis=0))
+    total = dot_nt(working[0], jnp.concatenate([third, zero], axis=0))
+    total = total + dot_nt(working[1], jnp.concatenate([zero, third], axis=0))
+    total = (total + (low[:, 128:] + high[:, 128:])) + (low[:, :128] + high[:, :128])
     gram = dot_nt(krylov, krylov, precision=highest)
     gram = jnp.concatenate([gram[:32], gram[32:]], axis=1)
     for i in range(FRM):
@@ -181,15 +212,20 @@
 def basis_kernel(gathered, krylov, projected_out, subspace_out, out, rows_ref):
     gram = jnp.concatenate([gathered[CHUNK * i + SLICE : CHUNK * i + CHUNK] for i in range(FRM)], axis=0)
     gram = jnp.concatenate([gram[:, :RANK], gram[:, RANK:]], axis=0)
-    for i, row in enumerate(eliminate(augment(gram), True)):
-        rows_ref[i : i + 1] = row[0:1]
+    for i, row in enumerate(factorize([[block] for block in augment(gram)])):
+        rows_ref[i : i + 1] = row[0][0:1]
     inverse = rows_ref[:, RANK:]
     zero = jnp.zeros((RANK, RANK), f32)
     pair = jnp.concatenate(
         [jnp.concatenate([inverse, zero], axis=1), jnp.concatenate([zero, inverse], axis=1)], axis=0
     )
     packed = jnp.concatenate([gathered[CHUNK * i : CHUNK * i + SLICE] for i in range(FRM)], axis=0)
-    projected = dot_nt(packed, pair, precision=highest)
+    left = split_three(packed)
+    right = split_three(pair)
+    outer = jnp.concatenate(right[:2], axis=0)
+    projected = dot_nt(jnp.concatenate(left[:2], axis=1), jnp.concatenate([outer, outer], axis=1))
+    rest = dot_nt(jnp.concatenate([left[0], left[2]], axis=1), jnp.concatenate([right[2], right[0]], axis=1))
+    projected = projected[:, :128] + (projected[:, 128:] + rest)
     projected_out[...] = projected
     subspace_out[...] = dot_nn(inverse, krylov[...], precision=highest)
     hi, lo = split_two(projected)
@@ -200,7 +236,7 @@
         out[32 * i : 32 * i + 32] = gram
 
 
-def finish_kernel(grams, subspace, video, multiplier, projected, sparse_out, multiplier_out, out, near, sems):
+def finish_kernel(grams, subspace, video, multiplier, projected, sparse_out, multiplier_out, out, near, rows_ref, sems):
     gram = grams[:32].astype(f32)
     for i in range(1, PIX):
         gram = gram + grams[32 * i : 32 * i + 32].astype(f32)
@@ -209,13 +245,16 @@
     cols = lax.broadcasted_iota(jnp.int32, (RANK, RANK), 1)
     eye = jnp.where(rows == cols, 1.0, 0.0).astype(f32)
     level = jnp.sum(jnp.sum(gram * eye, axis=0, keepdims=True), axis=1, keepdims=True) * (shrink_ratio / RANK)
-    blocks = eliminate(augment(gram + level * eye), False)
-    inverse = jnp.concatenate(blocks, axis=0)[:, RANK:]
-    weights = eye - level * inverse
-    mixed = dot_nn(weights, subspace[...], precision=highest)
+    wide = [subspace[8 * i : 8 * i + 8] for i in range(8)]
+    blocks = [[x, y[:, :128], y[:, 128:]] for x, y in zip(augment(gram + level * eye), wide)]
+    for i, row in enumerate(factorize(blocks)):
+        for j in range(3):
+            rows_ref[i : i + 1, 128 * j : 128 * j + 128] = row[j][0:1]
+    mixed = subspace[...] - level * dot_tn(rows_ref[:, RANK:128], rows_ref[:, 128:], precision=highest)
     zero = jnp.zeros((RANK, COLS), bf16)
     parts = split_two(mixed)
     weighted = [[jnp.concatenate(pair, axis=0) for pair in ((part, zero), (zero, part))] for part in parts]
+    weighted[0] = [jnp.concatenate([pair, pair], axis=0) for pair in weighted[0]]
 
     residual_sq = jnp.zeros((8, COLS), f32)
     video_sq = jnp.zeros((8, COLS), f32)
@@ -223,8 +262,9 @@
     for i in range(STEPS):
         rows = slice(TILE * i, TILE * i + TILE)
         hi, lo = split_two(projected[rows])
+        both = jnp.concatenate([hi, lo], axis=1)
         for h in range(2):
-            low_rank = dot_nn(hi, weighted[0][h]) + (dot_nn(hi, weighted[1][h]) + dot_nn(lo, weighted[0][h]))
+            low_rank = dot_nn(both, weighted[0][h]) + dot_nn(hi, weighted[1][h])
             video_full = video[h, rows].astype(f32)
             held = multiplier[h, rows]
             base = video_full - low_rank
@@ -325,7 +365,7 @@
         out_shape=(struct((2, HALF, COLS)), struct((2, HALF, COLS)), struct((PIX * 8, 128))),
         in_specs=[vmem] * 5,
         out_specs=(far, far, vmem),
-        scratch_shapes=[pltpu.VMEM((2, 2, HALF, COLS), f32), pltpu.SemaphoreType.DMA((4 * STEPS,))],
+        scratch_shapes=[pltpu.VMEM((2, 2, HALF, COLS), f32), pltpu.VMEM((RANK, 3 * 128), f32), pltpu.SemaphoreType.DMA((4 * STEPS,))],
         compiler_params=params,
     )(grams, subspace, video, multiplier, projected)
     sums = exchange(sums, "pix")

time: 132 us -> 131 us (level)
  Pallas kernels: 11.6 us -> 10.1 us
where the time goes in v3:
time: 131 us; the launch traced here: 130 us
  blocking collectives  120 us (92%)
  Pallas kernels  10.1 us (8%)
    all_to_all x8, blocking collectives, exchange(): return lax.all_to_all(x.reshape(parts), axis, 0, 0).reshape(x.shape)  120 us
    pallas_call x1, Pallas kernels, per_device(): pl.pallas_call(finish_kernel, out_shape=(struct((2, HALF, COLS)), struct(...  4 us

profile of v3, /device:TPU:1, one launch (start us, length us, event | category | flops | bytes accessed | tf_op | source)
XLA Modules:
  0.0 130.4 jit_solution(885165005668115640)
XLA Ops:
  0.6 2.0 %shard_map.67 = (bf16[2,512,256]{2,1,0:T(8,128)(2,1)S(1)}, bf16[512,128]{1,0:T(8,128)(2,1)S(1)}) custom-call(bf16[2,512,256]{2,1,0:T(8,128)(2,1)} %bitcast.25, f32[2,512,256]{2,1,0:T(8,128)} %bitcast.43, f32[2,512,256]{2,1,0:T(8,128)} %bitcast.23, bf16[64,256]{1,0:T(8,128)(2,1)} %bitcast.44), custom_call_target="tpu_custom_call" | custom-call | tf_op jit(solution)/shard_map/pallas_call | solution.py:325
  2.7 19.6 %all_to_all.40 = bf16[32,16,128]{2,1,0:T(8,128)(2,1)S(1)} all-to-all(bf16[32,16,128]{2,1,0:T(8,128)(2,1)S(1)} %bitcast.41), channel_id=1, replica_groups=mesh['pix'=16,'frm'=32] {'frm'}, dimensions={0} | all-to-all | bytes 262144 | tf_op jit(solution)/shard_map/all_to_all | solution.py:319
  22.4 12.6 %all_to_all.41 = bf16[32,16,128]{2,1,0:T(8,128)(2,1)S(1)} all-to-all(bf16[32,16,128]{2,1,0:T(8,128)(2,1)S(1)} %bitcast.32), channel_id=1, replica_groups=mesh['pix'=16,'frm'=32] {'frm'}, dimensions={0} | all-to-all | bytes 262144 | tf_op jit(solution)/shard_map/all_to_all | solution.py:319
  35.0 0.2 shard_map.69
  35.3 21.3 %all_to_all.42 = f32[16,1,1024]{2,1,0:T(1,128)S(1)} all-to-all(f32[16,1,1024]{2,1,0:T(1,128)S(1)} %bitcast.39), channel_id=1, replica_groups=mesh['pix'=16,'frm'=32] {'pix'}, dimensions={0} | all-to-all | bytes 131072 | tf_op jit(solution)/shard_map/all_to_all | solution.py:319
  56.5 10.4 %all_to_all.43 = f32[16,1,1024]{2,1,0:T(1,128)S(1)} all-to-all(f32[16,1,1024]{2,1,0:T(1,128)S(1)} %bitcast.37), channel_id=1, replica_groups=mesh['pix'=16,'frm'=32] {'pix'}, dimensions={0} | all-to-all | bytes 131072 | tf_op jit(solution)/shard_map/all_to_all | solution.py:319
  66.9 0.5 shard_map.71
  67.5 0.0 copy-start
  67.5 15.2 %all_to_all.44 = f32[32,1,2176]{2,1,0:T(1,128)S(1)} all-to-all(f32[32,1,2176]{2,1,0:T(1,128)S(1)} %bitcast.34), channel_id=1, replica_groups=mesh['pix'=16,'frm'=32] {'frm'}, dimensions={0} | all-to-all | bytes 557056 | tf_op jit(solution)/shard_map/all_to_all | solution.py:319
  82.7 0.1 shard_map.72
  82.8 0.0 copy-start.1
  82.8 15.0 %all_to_all.45 = f32[32,1,2176]{2,1,0:T(1,128)S(1)} all-to-all(f32[32,1,2176]{2,1,0:T(1,128)S(1)} %bitcast.29), channel_id=1, replica_groups=mesh['pix'=16,'frm'=32] {'frm'}, dimensions={0} | all-to-all | bytes 557056 | tf_op jit(solution)/shard_map/all_to_all | solution.py:319
  97.8 2.6 %shard_map.73 = (f32[512,128]{1,0:T(8,128)S(1)}, f32[64,256]{1,0:T(8,128)S(1)}, bf16[512,128]{1,0:T(8,128)(2,1)S(1)}) custom-call(f32[544,128]{1,0:T(8,128)S(1)} %bitcast.27, f32[64,256]{1,0:T(8,128)S(1)} %get-tuple-element.16.krylov), custom_call_target="tpu_custom_call" | custom-call | tf_op jit(solution)/shard_map/pallas_call | solution.py:355
  100.4 15.1 %all_to_all.46 = bf16[16,32,128]{2,1,0:T(8,128)(2,1)S(1)} all-to-all(bf16[16,32,128]{2,1,0:T(8,128)(2,1)S(1)} %bitcast.40), channel_id=1, replica_groups=mesh['pix'=16,'frm'=32] {'pix'}, dimensions={0} | all-to-all | bytes 262144 | tf_op jit(solution)/shard_map/all_to_all | solution.py:319
  115.5 0.0 copy-done
  115.5 0.0 copy-done.1
  115.5 4.0 %shard_map.74 = (f32[2,512,256]{2,1,0:T(8,128)}, f32[2,512,256]{2,1,0:T(8,128)}, f32[128,128]{1,0:T(8,128)S(1)}) custom-call(bf16[512,128]{1,0:T(8,128)(2,1)S(1)} %bitcast.30, f32[64,256]{1,0:T(8,128)S(1)} %get-tuple-element.18.subspace, bf16[2,512,256]{2,1,0:T(8,128)(2,1)S(1)} %bitcast.26, f32[2,512,256]{2,1,0:T(8,128)S(1)} %bitcast.24, ...), custom_call_target="tpu_custom_call" | custom-call | tf_op jit(solution)/shard_map/pallas_call | solution.py:363
  119.5 10.2 %all_to_all.47 = f32[16,1,1024]{2,1,0:T(1,128)S(1)} all-to-all(f32[16,1,1024]{2,1,0:T(1,128)S(1)} %bitcast.42), channel_id=1, replica_groups=mesh['pix'=16,'frm'=32] {'pix'}, dimensions={0} | all-to-all | bytes 131072 | tf_op jit(solution)/shard_map/all_to_all | solution.py:319
  129.8 0.6 shard_map.75
  (2 shorter events, 0.1 us)
Async XLA Ops:
  67.5 48.0 %copy-start = (f32[1024,256]{1,0:T(8,128)S(1)}, f32[1024,256]{1,0:T(8,128)}, u32[]{:S(2)}) copy-start(f32[1024,256]{1,0:T(8,128)} %param.6) | copy-start | bytes 3145732
  82.8 32.7 %copy-start.1 = (bf16[1024,256]{1,0:T(8,128)(2,1)S(1)}, bf16[1024,256]{1,0:T(8,128)(2,1)}, u32[]{:S(2)}) copy-start(bf16[1024,256]{1,0:T(8,128)(2,1)} %param.4) | copy-start | bytes 1572868

commit v4 on v3

--- a/solution.py
+++ b/solution.py
@@ -282,19 +282,19 @@
     residual_sq = jnp.sum(residual_sq, axis=0, keepdims=True)
     video_sq = jnp.sum(video_sq, axis=0, keepdims=True)
     tile = jnp.concatenate(
-        [residual_sq[:, :128], residual_sq[:, 128:], video_sq[:, :128], video_sq[:, 128:], jnp.zeros((4, 128), f32)],
+        [residual_sq[:, :128], residual_sq[:, 128:], video_sq[:, :128], video_sq[:, 128:]],
         axis=0,
     )
     for i in range(PIX):
-        out[8 * i : 8 * i + 8] = tile
+        out[4 * i : 4 * i + 4] = tile
     for copy in copies:
         copy.wait()
 
 
 def ratio_kernel(x, out):
-    total = x[:8]
+    total = x[:4]
     for i in range(1, PIX):
-        total = total + x[8 * i : 8 * i + 8]
+        total = total + x[4 * i : 4 * i + 4]
     out[...] = jnp.sqrt(total[0:2] / (total[2:4] + epsilon_value))
 
 
@@ -316,7 +316,9 @@
 def exchange(x, axis):
     peers = FRM if axis == "frm" else PIX
     parts = (peers, 1, -1) if x.dtype == f32 else (peers, -1, 128)
-    return lax.all_to_all(x.reshape(parts), axis, 0, 0).reshape(x.shape)
+    index = [[p * FRM + f for f in range(FRM)] for p in range(PIX)]
+    groups = index if axis == "frm" else [list(group) for group in zip(*index)]
+    return lax.all_to_all(x.reshape(parts), ("pix", "frm"), 0, 0, axis_index_groups=groups).reshape(x.shape)
 
 
 def per_device(video, sparse, multiplier, start_block):
@@ -362,7 +364,7 @@
 
     sparse_next, multiplier_next, sums = pl.pallas_call(
         finish_kernel,
-        out_shape=(struct((2, HALF, COLS)), struct((2, HALF, COLS)), struct((PIX * 8, 128))),
+        out_shape=(struct((2, HALF, COLS)), struct((2, HALF, COLS)), struct((PIX * 4, 128))),
         in_specs=[vmem] * 5,
         out_specs=(far, far, vmem),
         scratch_shapes=[pltpu.VMEM((2, 2, HALF, COLS), f32), pltpu.VMEM((RANK, 3 * 128), f32), pltpu.SemaphoreType.DMA((4 * STEPS,))],

time: 131 us -> 130 us (level)
  no operation moved by 1% of the time
where the time goes in v4:
time: 130 us
  blocking collectives  119 us (92%)
  Pallas kernels  10.1 us (8%)
    all_to_all x8, blocking collectives, exchange(): lax.all_to_all(x.reshape(parts), ('pix', 'frm'), 0, 0, axis_index_groups=...  119 us
    pallas_call x1, Pallas kernels, per_device(): pl.pallas_call(finish_kernel, out_shape=(struct((2, HALF, COLS)), struct(...  4 us

profile of v4, /device:TPU:1, one launch (start us, length us, event | category | flops | bytes accessed | tf_op | source)
XLA Modules:
  0.0 130.0 jit_solution(8394396163398973637)
XLA Ops:
  0.6 2.0 %shard_map.67 = (bf16[2,512,256]{2,1,0:T(8,128)(2,1)S(1)}, bf16[512,128]{1,0:T(8,128)(2,1)S(1)}) custom-call(bf16[2,512,256]{2,1,0:T(8,128)(2,1)} %bitcast.25, f32[2,512,256]{2,1,0:T(8,128)} %bitcast.43, f32[2,512,256]{2,1,0:T(8,128)} %bitcast.23, bf16[64,256]{1,0:T(8,128)(2,1)} %bitcast.44), custom_call_target="tpu_custom_call" | custom-call | tf_op jit(solution)/shard_map/pallas_call | solution.py:327
  2.7 19.6 %all_to_all.40 = bf16[32,16,128]{2,1,0:T(8,128)(2,1)S(1)} all-to-all(bf16[32,16,128]{2,1,0:T(8,128)(2,1)S(1)} %bitcast.40), channel_id=1, replica_groups={{0,1,2,3,4,5,6,7,8,9,10,11,12,13,14,15,16,17,18,19,20,21,22,23,24,25,26..., dimensions={0} | all-to-all | bytes 262144 | tf_op jit(solution)/shard_map/all_to_all | solution.py:321
  22.4 12.6 %all_to_all.41 = bf16[32,16,128]{2,1,0:T(8,128)(2,1)S(1)} all-to-all(bf16[32,16,128]{2,1,0:T(8,128)(2,1)S(1)} %bitcast.32), channel_id=1, replica_groups={{0,1,2,3,4,5,6,7,8,9,10,11,12,13,14,15,16,17,18,19,20,21,22,23,24,25,26..., dimensions={0} | all-to-all | bytes 262144 | tf_op jit(solution)/shard_map/all_to_all | solution.py:321
  35.0 0.2 shard_map.69
  35.3 21.3 %all_to_all.42 = f32[16,1,1024]{2,1,0:T(1,128)S(1)} all-to-all(f32[16,1,1024]{2,1,0:T(1,128)S(1)} %bitcast.38), channel_id=1, replica_groups={{0,32,64,96,128,160,192,224,256,288,320,352,384,416,448,480},{1,33,65,9..., dimensions={0} | all-to-all | bytes 131072 | tf_op jit(solution)/shard_map/all_to_all | solution.py:321
  56.5 10.4 %all_to_all.43 = f32[16,1,1024]{2,1,0:T(1,128)S(1)} all-to-all(f32[16,1,1024]{2,1,0:T(1,128)S(1)} %bitcast.37), channel_id=1, replica_groups={{0,32,64,96,128,160,192,224,256,288,320,352,384,416,448,480},{1,33,65,9..., dimensions={0} | all-to-all | bytes 131072 | tf_op jit(solution)/shard_map/all_to_all | solution.py:321
  66.9 0.5 shard_map.71
  67.5 0.0 copy-start
  67.5 15.2 %all_to_all.44 = f32[32,1,2176]{2,1,0:T(1,128)S(1)} all-to-all(f32[32,1,2176]{2,1,0:T(1,128)S(1)} %bitcast.34), channel_id=1, replica_groups={{0,1,2,3,4,5,6,7,8,9,10,11,12,13,14,15,16,17,18,19,20,21,22,23,24,25,26..., dimensions={0} | all-to-all | bytes 557056 | tf_op jit(solution)/shard_map/all_to_all | solution.py:321
  82.7 0.1 shard_map.72
  82.8 0.0 copy-start.1
  82.8 15.0 %all_to_all.45 = f32[32,1,2176]{2,1,0:T(1,128)S(1)} all-to-all(f32[32,1,2176]{2,1,0:T(1,128)S(1)} %bitcast.29), channel_id=1, replica_groups={{0,1,2,3,4,5,6,7,8,9,10,11,12,13,14,15,16,17,18,19,20,21,22,23,24,25,26..., dimensions={0} | all-to-all | bytes 557056 | tf_op jit(solution)/shard_map/all_to_all | solution.py:321
  97.8 2.6 %shard_map.73 = (f32[512,128]{1,0:T(8,128)S(1)}, f32[64,256]{1,0:T(8,128)S(1)}, bf16[512,128]{1,0:T(8,128)(2,1)S(1)}) custom-call(f32[544,128]{1,0:T(8,128)S(1)} %bitcast.27, f32[64,256]{1,0:T(8,128)S(1)} %get-tuple-element.16.krylov), custom_call_target="tpu_custom_call" | custom-call | tf_op jit(solution)/shard_map/pallas_call | solution.py:357
  100.4 15.1 %all_to_all.46 = bf16[16,32,128]{2,1,0:T(8,128)(2,1)S(1)} all-to-all(bf16[16,32,128]{2,1,0:T(8,128)(2,1)S(1)} %bitcast.39), channel_id=1, replica_groups={{0,32,64,96,128,160,192,224,256,288,320,352,384,416,448,480},{1,33,65,9..., dimensions={0} | all-to-all | bytes 262144 | tf_op jit(solution)/shard_map/all_to_all | solution.py:321
  115.5 0.0 copy-done
  115.5 0.0 copy-done.1
  115.5 4.0 %shard_map.74 = (f32[2,512,256]{2,1,0:T(8,128)}, f32[2,512,256]{2,1,0:T(8,128)}, f32[64,128]{1,0:T(8,128)S(1)}) custom-call(bf16[512,128]{1,0:T(8,128)(2,1)S(1)} %bitcast.30, f32[64,256]{1,0:T(8,128)S(1)} %get-tuple-element.18.subspace, bf16[2,512,256]{2,1,0:T(8,128)(2,1)S(1)} %bitcast.26, f32[2,512,256]{2,1,0:T(8,128)S(1)} %bitcast.24, ...), custom_call_target="tpu_custom_call" | custom-call | tf_op jit(solution)/shard_map/pallas_call | solution.py:365
  119.5 9.8 %all_to_all.47 = f32[16,1,512]{2,1,0:T(1,128)S(1)} all-to-all(f32[16,1,512]{2,1,0:T(1,128)S(1)} %bitcast.42), channel_id=1, replica_groups={{0,32,64,96,128,160,192,224,256,288,320,352,384,416,448,480},{1,33,65,9..., dimensions={0} | all-to-all | bytes 65536 | tf_op jit(solution)/shard_map/all_to_all | solution.py:321
  129.4 0.6 shard_map.75
  (2 shorter events, 0.1 us)
Async XLA Ops:
  67.5 48.0 %copy-start = (f32[1024,256]{1,0:T(8,128)S(1)}, f32[1024,256]{1,0:T(8,128)}, u32[]{:S(2)}) copy-start(f32[1024,256]{1,0:T(8,128)} %param.6) | copy-start | bytes 3145732
  82.8 32.7 %copy-start.1 = (bf16[1024,256]{1,0:T(8,128)(2,1)S(1)}, bf16[1024,256]{1,0:T(8,128)(2,1)}, u32[]{:S(2)}) copy-start(bf16[1024,256]{1,0:T(8,128)(2,1)} %param.4) | copy-start | bytes 1572868

commit v5 on v4

--- a/solution.py
+++ b/solution.py
@@ -147,6 +147,26 @@
     return rows
 
 
+def pack_symmetric(gram):
+    wide = jnp.concatenate([gram[:32], gram[32:]], axis=1)
+    free = (lane_iota() >= 64) & (lane_iota() < 96)
+    tail = wide[24:]
+    return jnp.concatenate(
+        [jnp.where(free, pltpu.roll(tail, shift, 1), wide[8 * i : 8 * i + 8]) for i, shift in enumerate((64, 32, 96))],
+        axis=0,
+    )
+
+
+def unpack_symmetric(packed):
+    lane = lane_iota()
+    first, second, third = (pltpu.roll(packed[8 * i : 8 * i + 8], shift, 1) for i, shift in enumerate((64, 96, 32)))
+    tail = jnp.where(lane < 32, first, jnp.where(lane < 64, second, third))
+    wide = jnp.concatenate([packed, tail], axis=0)
+    upper = wide[:, :64]
+    lower = jnp.concatenate([upper[:, 32:].T, wide[:, 96:]], axis=1)
+    return jnp.concatenate([upper, lower], axis=0)
+
+
 def start_kernel(video, sparse, multiplier, start, working, across, video_in, sparse_in, multiplier_in, start_in, sems):
     sources = ((video, video_in), (sparse, sparse_in), (multiplier, multiplier_in))
     copies = [pltpu.make_async_copy(start, start_in, sems.at[3 * START_STEPS])]
@@ -231,16 +251,16 @@
     hi, lo = split_two(projected)
     gram = dot_tn(hi, hi) + (dot_tn(hi, lo) + dot_tn(lo, hi))
     gram = gram[:RANK, :RANK] + gram[RANK:, RANK:]
-    gram = jnp.concatenate([gram[:32], gram[32:]], axis=1).astype(bf16)
+    gram = pack_symmetric(gram).astype(bf16)
     for i in range(PIX):
-        out[32 * i : 32 * i + 32] = gram
+        out[i] = gram
 
 
 def finish_kernel(grams, subspace, video, multiplier, projected, sparse_out, multiplier_out, out, near, rows_ref, sems):
-    gram = grams[:32].astype(f32)
+    gram = grams[0].astype(f32)
     for i in range(1, PIX):
-        gram = gram + grams[32 * i : 32 * i + 32].astype(f32)
-    gram = jnp.concatenate([gram[:, :RANK], gram[:, RANK:]], axis=0)
+        gram = gram + grams[i].astype(f32)
+    gram = unpack_symmetric(gram)
     rows = lax.broadcasted_iota(jnp.int32, (RANK, RANK), 0)
     cols = lax.broadcasted_iota(jnp.int32, (RANK, RANK), 1)
     eye = jnp.where(rows == cols, 1.0, 0.0).astype(f32)
@@ -356,7 +376,7 @@
 
     projected, subspace, grams = whole(
         basis_kernel,
-        (struct((HALF, 128)), struct((RANK, COLS)), struct((PIX * 32, 128), bf16)),
+        (struct((HALF, 128)), struct((RANK, COLS)), struct((PIX, 24, 128), bf16)),
         2,
         scratch_shapes=[pltpu.VMEM((RANK, 128), f32)],
     )(projected, krylov)

time: 130 us -> 130 us (level)
  no operation moved by 1% of the time
where the time goes in v5:
time: 130 us; the launch traced here: 129 us
  blocking collectives  118 us (91%)
  Pallas kernels  10.3 us (8%)
    all_to_all x8, blocking collectives, exchange(): lax.all_to_all(x.reshape(parts), ('pix', 'frm'), 0, 0, axis_index_groups=...  118 us
    pallas_call x1, Pallas kernels, per_device(): pl.pallas_call(finish_kernel, out_shape=(struct((2, HALF, COLS)), struct(...  4.14 us
    pallas_call x1, Pallas kernels, per_device(): whole(basis_kernel, (struct((HALF, 128)), struct((RANK, COLS)), struct((P...  2.65 us

profile of v5, /device:TPU:1, one launch (start us, length us, event | category | flops | bytes accessed | tf_op | source)
XLA Modules:
  0.0 129.4 jit_solution(5157789192156203413)
XLA Ops:
  0.6 2.0 %shard_map.67 = (bf16[2,512,256]{2,1,0:T(8,128)(2,1)S(1)}, bf16[512,128]{1,0:T(8,128)(2,1)S(1)}) custom-call(bf16[2,512,256]{2,1,0:T(8,128)(2,1)} %bitcast.23, f32[2,512,256]{2,1,0:T(8,128)} %bitcast.39, f32[2,512,256]{2,1,0:T(8,128)} %bitcast.21, bf16[64,256]{1,0:T(8,128)(2,1)} %bitcast.40), custom_call_target="tpu_custom_call" | custom-call | tf_op jit(solution)/shard_map/pallas_call | solution.py:347
  2.7 19.6 %all_to_all.40 = bf16[32,16,128]{2,1,0:T(8,128)(2,1)S(1)} all-to-all(bf16[32,16,128]{2,1,0:T(8,128)(2,1)S(1)} %bitcast.36), channel_id=1, replica_groups={{0,1,2,3,4,5,6,7,8,9,10,11,12,13,14,15,16,17,18,19,20,21,22,23,24,25,26..., dimensions={0} | all-to-all | bytes 262144 | tf_op jit(solution)/shard_map/all_to_all | solution.py:341
  22.4 12.6 %all_to_all.41 = bf16[32,16,128]{2,1,0:T(8,128)(2,1)S(1)} all-to-all(bf16[32,16,128]{2,1,0:T(8,128)(2,1)S(1)} %bitcast.29), channel_id=1, replica_groups={{0,1,2,3,4,5,6,7,8,9,10,11,12,13,14,15,16,17,18,19,20,21,22,23,24,25,26..., dimensions={0} | all-to-all | bytes 262144 | tf_op jit(solution)/shard_map/all_to_all | solution.py:341
  35.0 0.2 shard_map.69
  35.3 21.3 %all_to_all.42 = f32[16,1,1024]{2,1,0:T(1,128)S(1)} all-to-all(f32[16,1,1024]{2,1,0:T(1,128)S(1)} %bitcast.35), channel_id=1, replica_groups={{0,32,64,96,128,160,192,224,256,288,320,352,384,416,448,480},{1,33,65,9..., dimensions={0} | all-to-all | bytes 131072 | tf_op jit(solution)/shard_map/all_to_all | solution.py:341
  56.5 10.4 %all_to_all.43 = f32[16,1,1024]{2,1,0:T(1,128)S(1)} all-to-all(f32[16,1,1024]{2,1,0:T(1,128)S(1)} %bitcast.34), channel_id=1, replica_groups={{0,32,64,96,128,160,192,224,256,288,320,352,384,416,448,480},{1,33,65,9..., dimensions={0} | all-to-all | bytes 131072 | tf_op jit(solution)/shard_map/all_to_all | solution.py:341
  66.9 0.5 shard_map.71
  67.5 0.0 copy-start
  67.5 15.2 %all_to_all.44 = f32[32,1,2176]{2,1,0:T(1,128)S(1)} all-to-all(f32[32,1,2176]{2,1,0:T(1,128)S(1)} %bitcast.31), channel_id=1, replica_groups={{0,1,2,3,4,5,6,7,8,9,10,11,12,13,14,15,16,17,18,19,20,21,22,23,24,25,26..., dimensions={0} | all-to-all | bytes 557056 | tf_op jit(solution)/shard_map/all_to_all | solution.py:341
  82.7 0.1 shard_map.72
  82.8 0.0 copy-start.1
  82.8 15.0 %all_to_all.45 = f32[32,1,2176]{2,1,0:T(1,128)S(1)} all-to-all(f32[32,1,2176]{2,1,0:T(1,128)S(1)} %bitcast.27), channel_id=1, replica_groups={{0,1,2,3,4,5,6,7,8,9,10,11,12,13,14,15,16,17,18,19,20,21,22,23,24,25,26..., dimensions={0} | all-to-all | bytes 557056 | tf_op jit(solution)/shard_map/all_to_all | solution.py:341
  97.8 2.7 %shard_map.73 = (f32[512,128]{1,0:T(8,128)S(1)}, f32[64,256]{1,0:T(8,128)S(1)}, bf16[16,24,128]{2,1,0:T(8,128)(2,1)S(1)}) custom-call(f32[544,128]{1,0:T(8,128)S(1)} %bitcast.25, f32[64,256]{1,0:T(8,128)S(1)} %get-tuple-element.16.krylov), custom_call_target="tpu_custom_call" | custom-call | tf_op jit(solution)/shard_map/pallas_call | solution.py:377
  100.5 14.4 %all_to_all.46.grams = bf16[16,24,128]{2,1,0:T(8,128)(2,1)S(1)} all-to-all(bf16[16,24,128]{2,1,0:T(8,128)(2,1)S(1)} %get-tuple-element.17), channel_id=1, replica_groups={{0,32,64,96,128,160,192,224,256,288,320,352,384,416,448,480},{1,33,65,9..., dimensions={0} | all-to-all | bytes 196608 | tf_op jit(solution)/shard_map/all_to_all | solution.py:341
  114.9 0.0 copy-done
  114.9 0.0 copy-done.1
  114.9 4.1 %shard_map.74 = (f32[2,512,256]{2,1,0:T(8,128)}, f32[2,512,256]{2,1,0:T(8,128)}, f32[64,128]{1,0:T(8,128)S(1)}) custom-call(bf16[16,24,128]{2,1,0:T(8,128)(2,1)S(1)} %all_to_all.46.grams, f32[64,256]{1,0:T(8,128)S(1)} %get-tuple-element.18.subspace, bf16[2,512,256]{2,1,0:T(8,128)(2,1)S(1)} %bitcast.24, f32[2,512,256]{2,1,0:T(8,128)S(1)} %bitcast.22, ...), custom_call_target="tpu_custom_call" | custom-call | tf_op jit(solution)/shard_map/pallas_call | solution.py:385
  119.1 9.8 %all_to_all.47 = f32[16,1,512]{2,1,0:T(1,128)S(1)} all-to-all(f32[16,1,512]{2,1,0:T(1,128)S(1)} %bitcast.38), channel_id=1, replica_groups={{0,32,64,96,128,160,192,224,256,288,320,352,384,416,448,480},{1,33,65,9..., dimensions={0} | all-to-all | bytes 65536 | tf_op jit(solution)/shard_map/all_to_all | solution.py:341
  128.8 0.6 shard_map.75
  (2 shorter events, 0.1 us)
Async XLA Ops:
  67.5 47.4 %copy-start = (f32[1024,256]{1,0:T(8,128)S(1)}, f32[1024,256]{1,0:T(8,128)}, u32[]{:S(2)}) copy-start(f32[1024,256]{1,0:T(8,128)} %param.6) | copy-start | bytes 3145732
  82.8 32.1 %copy-start.1 = (bf16[1024,256]{1,0:T(8,128)(2,1)S(1)}, bf16[1024,256]{1,0:T(8,128)(2,1)}, u32[]{:S(2)}) copy-start(bf16[1024,256]{1,0:T(8,128)(2,1)} %param.4) | copy-start | bytes 1572868

commit v6 on v5

--- a/solution.py
+++ b/solution.py
@@ -249,8 +249,10 @@
     projected_out[...] = projected
     subspace_out[...] = dot_nn(inverse, krylov[...], precision=highest)
     hi, lo = split_two(projected)
-    gram = dot_tn(hi, hi) + (dot_tn(hi, lo) + dot_tn(lo, hi))
-    gram = gram[:RANK, :RANK] + gram[RANK:, RANK:]
+    gram = dot_tn(hi, jnp.concatenate([hi, lo], axis=1))
+    gram = gram[:RANK] + jnp.concatenate([pltpu.roll(gram[RANK:, :128], 64, 1), pltpu.roll(gram[RANK:, 128:], 64, 1)], axis=1)
+    rest = gram[:, 128 : 128 + RANK]
+    gram = gram[:, :RANK] + (rest + rest.T)
     gram = pack_symmetric(gram).astype(bf16)
     for i in range(PIX):
         out[i] = gram

time: 130 us -> 130 us (level)
  no operation moved by 1% of the time
where the time goes in v6:
time: 130 us; the launch traced here: 129 us
  blocking collectives  118 us (91%)
  Pallas kernels  10.3 us (8%)
    all_to_all x8, blocking collectives, exchange(): lax.all_to_all(x.reshape(parts), ('pix', 'frm'), 0, 0, axis_index_groups=...  118 us
    pallas_call x1, Pallas kernels, per_device(): pl.pallas_call(finish_kernel, out_shape=(struct((2, HALF, COLS)), struct(...  4.14 us
    pallas_call x1, Pallas kernels, per_device(): whole(basis_kernel, (struct((HALF, 128)), struct((RANK, COLS)), struct((P...  2.63 us

profile of v6, /device:TPU:1, one launch (start us, length us, event | category | flops | bytes accessed | tf_op | source)
XLA Modules:
  0.0 129.4 jit_solution(6952798884301634103)
XLA Ops:
  0.6 2.0 %shard_map.67 = (bf16[2,512,256]{2,1,0:T(8,128)(2,1)S(1)}, bf16[512,128]{1,0:T(8,128)(2,1)S(1)}) custom-call(bf16[2,512,256]{2,1,0:T(8,128)(2,1)} %bitcast.23, f32[2,512,256]{2,1,0:T(8,128)} %bitcast.39, f32[2,512,256]{2,1,0:T(8,128)} %bitcast.21, bf16[64,256]{1,0:T(8,128)(2,1)} %bitcast.40), custom_call_target="tpu_custom_call" | custom-call | tf_op jit(solution)/shard_map/pallas_call | solution.py:349
  2.7 19.6 %all_to_all.40 = bf16[32,16,128]{2,1,0:T(8,128)(2,1)S(1)} all-to-all(bf16[32,16,128]{2,1,0:T(8,128)(2,1)S(1)} %bitcast.36), channel_id=1, replica_groups={{0,1,2,3,4,5,6,7,8,9,10,11,12,13,14,15,16,17,18,19,20,21,22,23,24,25,26..., dimensions={0} | all-to-all | bytes 262144 | tf_op jit(solution)/shard_map/all_to_all | solution.py:343
  22.4 12.6 %all_to_all.41 = bf16[32,16,128]{2,1,0:T(8,128)(2,1)S(1)} all-to-all(bf16[32,16,128]{2,1,0:T(8,128)(2,1)S(1)} %bitcast.29), channel_id=1, replica_groups={{0,1,2,3,4,5,6,7,8,9,10,11,12,13,14,15,16,17,18,19,20,21,22,23,24,25,26..., dimensions={0} | all-to-all | bytes 262144 | tf_op jit(solution)/shard_map/all_to_all | solution.py:343
  35.0 0.2 shard_map.69
  35.3 21.3 %all_to_all.42 = f32[16,1,1024]{2,1,0:T(1,128)S(1)} all-to-all(f32[16,1,1024]{2,1,0:T(1,128)S(1)} %bitcast.35), channel_id=1, replica_groups={{0,32,64,96,128,160,192,224,256,288,320,352,384,416,448,480},{1,33,65,9..., dimensions={0} | all-to-all | bytes 131072 | tf_op jit(solution)/shard_map/all_to_all | solution.py:343
  56.5 10.4 %all_to_all.43 = f32[16,1,1024]{2,1,0:T(1,128)S(1)} all-to-all(f32[16,1,1024]{2,1,0:T(1,128)S(1)} %bitcast.34), channel_id=1, replica_groups={{0,32,64,96,128,160,192,224,256,288,320,352,384,416,448,480},{1,33,65,9..., dimensions={0} | all-to-all | bytes 131072 | tf_op jit(solution)/shard_map/all_to_all | solution.py:343
  66.9 0.5 shard_map.71
  67.5 0.0 copy-start
  67.5 15.2 %all_to_all.44 = f32[32,1,2176]{2,1,0:T(1,128)S(1)} all-to-all(f32[32,1,2176]{2,1,0:T(1,128)S(1)} %bitcast.31), channel_id=1, replica_groups={{0,1,2,3,4,5,6,7,8,9,10,11,12,13,14,15,16,17,18,19,20,21,22,23,24,25,26..., dimensions={0} | all-to-all | bytes 557056 | tf_op jit(solution)/shard_map/all_to_all | solution.py:343
  82.7 0.1 shard_map.72
  82.8 0.0 copy-start.1
  82.8 15.0 %all_to_all.45 = f32[32,1,2176]{2,1,0:T(1,128)S(1)} all-to-all(f32[32,1,2176]{2,1,0:T(1,128)S(1)} %bitcast.27), channel_id=1, replica_groups={{0,1,2,3,4,5,6,7,8,9,10,11,12,13,14,15,16,17,18,19,20,21,22,23,24,25,26..., dimensions={0} | all-to-all | bytes 557056 | tf_op jit(solution)/shard_map/all_to_all | solution.py:343
  97.8 2.6 %shard_map.73 = (f32[512,128]{1,0:T(8,128)S(1)}, f32[64,256]{1,0:T(8,128)S(1)}, bf16[16,24,128]{2,1,0:T(8,128)(2,1)S(1)}) custom-call(f32[544,128]{1,0:T(8,128)S(1)} %bitcast.25, f32[64,256]{1,0:T(8,128)S(1)} %get-tuple-element.16.krylov), custom_call_target="tpu_custom_call" | custom-call | tf_op jit(solution)/shard_map/pallas_call | solution.py:379
  100.5 14.4 %all_to_all.46.grams = bf16[16,24,128]{2,1,0:T(8,128)(2,1)S(1)} all-to-all(bf16[16,24,128]{2,1,0:T(8,128)(2,1)S(1)} %get-tuple-element.17), channel_id=1, replica_groups={{0,32,64,96,128,160,192,224,256,288,320,352,384,416,448,480},{1,33,65,9..., dimensions={0} | all-to-all | bytes 196608 | tf_op jit(solution)/shard_map/all_to_all | solution.py:343
  114.9 0.0 copy-done
  114.9 0.0 copy-done.1
  114.9 4.1 %shard_map.74 = (f32[2,512,256]{2,1,0:T(8,128)}, f32[2,512,256]{2,1,0:T(8,128)}, f32[64,128]{1,0:T(8,128)S(1)}) custom-call(bf16[16,24,128]{2,1,0:T(8,128)(2,1)S(1)} %all_to_all.46.grams, f32[64,256]{1,0:T(8,128)S(1)} %get-tuple-element.18.subspace, bf16[2,512,256]{2,1,0:T(8,128)(2,1)S(1)} %bitcast.24, f32[2,512,256]{2,1,0:T(8,128)S(1)} %bitcast.22, ...), custom_call_target="tpu_custom_call" | custom-call | tf_op jit(solution)/shard_map/pallas_call | solution.py:387
  119.0 9.8 %all_to_all.47 = f32[16,1,512]{2,1,0:T(1,128)S(1)} all-to-all(f32[16,1,512]{2,1,0:T(1,128)S(1)} %bitcast.38), channel_id=1, replica_groups={{0,32,64,96,128,160,192,224,256,288,320,352,384,416,448,480},{1,33,65,9..., dimensions={0} | all-to-all | bytes 65536 | tf_op jit(solution)/shard_map/all_to_all | solution.py:343
  128.8 0.6 shard_map.75
  (2 shorter events, 0.1 us)
Async XLA Ops:
  67.5 47.4 %copy-start = (f32[1024,256]{1,0:T(8,128)S(1)}, f32[1024,256]{1,0:T(8,128)}, u32[]{:S(2)}) copy-start(f32[1024,256]{1,0:T(8,128)} %param.6) | copy-start | bytes 3145732
  82.8 32.1 %copy-start.1 = (bf16[1024,256]{1,0:T(8,128)(2,1)S(1)}, bf16[1024,256]{1,0:T(8,128)(2,1)}, u32[]{:S(2)}) copy-start(bf16[1024,256]{1,0:T(8,128)(2,1)} %param.4) | copy-start | bytes 1572868

commit v7 on v5

--- a/solution.py
+++ b/solution.py
@@ -164,7 +164,11 @@
     wide = jnp.concatenate([packed, tail], axis=0)
     upper = wide[:, :64]
     lower = jnp.concatenate([upper[:, 32:].T, wide[:, 96:]], axis=1)
-    return jnp.concatenate([upper, lower], axis=0)
+    row = lax.broadcasted_iota(jnp.int32, (32, 128), 0)
+    lane = lax.broadcasted_iota(jnp.int32, (32, 128), 1)
+    diagonal = jnp.where((lane == row) | (lane == row + 96), wide, 0.0)
+    trace = jnp.sum(jnp.sum(diagonal, axis=0, keepdims=True), axis=1, keepdims=True)
+    return jnp.concatenate([upper, lower], axis=0), trace
 
 
 def start_kernel(video, sparse, multiplier, start, working, across, video_in, sparse_in, multiplier_in, start_in, sems):
@@ -260,11 +264,11 @@
     gram = grams[0].astype(f32)
     for i in range(1, PIX):
         gram = gram + grams[i].astype(f32)
-    gram = unpack_symmetric(gram)
+    gram, trace = unpack_symmetric(gram)
     rows = lax.broadcasted_iota(jnp.int32, (RANK, RANK), 0)
     cols = lax.broadcasted_iota(jnp.int32, (RANK, RANK), 1)
     eye = jnp.where(rows == cols, 1.0, 0.0).astype(f32)
-    level = jnp.sum(jnp.sum(gram * eye, axis=0, keepdims=True), axis=1, keepdims=True) * (shrink_ratio / RANK)
+    level = trace * (shrink_ratio / RANK)
     wide = [subspace[8 * i : 8 * i + 8] for i in range(8)]
     blocks = [[x, y[:, :128], y[:, 128:]] for x, y in zip(augment(gram + level * eye), wide)]
     for i, row in enumerate(factorize(blocks)):

time: 130 us -> 130 us (level)
  no operation moved by 1% of the time
where the time goes in v7:
time: 130 us; the launch traced here: 129 us
  blocking collectives  118 us (91%)
  Pallas kernels  10.3 us (8%)
    all_to_all x8, blocking collectives, exchange(): lax.all_to_all(x.reshape(parts), ('pix', 'frm'), 0, 0, axis_index_groups=...  118 us
    pallas_call x1, Pallas kernels, per_device(): pl.pallas_call(finish_kernel, out_shape=(struct((2, HALF, COLS)), struct(...  4.09 us
    pallas_call x1, Pallas kernels, per_device(): whole(basis_kernel, (struct((HALF, 128)), struct((RANK, COLS)), struct((P...  2.65 us

profile of v7, /device:TPU:1, one launch (start us, length us, event | category | flops | bytes accessed | tf_op | source)
XLA Modules:
  0.0 129.4 jit_solution(5883666850273024166)
XLA Ops:
  0.6 2.0 %shard_map.67 = (bf16[2,512,256]{2,1,0:T(8,128)(2,1)S(1)}, bf16[512,128]{1,0:T(8,128)(2,1)S(1)}) custom-call(bf16[2,512,256]{2,1,0:T(8,128)(2,1)} %bitcast.23, f32[2,512,256]{2,1,0:T(8,128)} %bitcast.39, f32[2,512,256]{2,1,0:T(8,128)} %bitcast.21, bf16[64,256]{1,0:T(8,128)(2,1)} %bitcast.40), custom_call_target="tpu_custom_call" | custom-call | tf_op jit(solution)/shard_map/pallas_call | solution.py:351
  2.7 19.6 %all_to_all.40 = bf16[32,16,128]{2,1,0:T(8,128)(2,1)S(1)} all-to-all(bf16[32,16,128]{2,1,0:T(8,128)(2,1)S(1)} %bitcast.36), channel_id=1, replica_groups={{0,1,2,3,4,5,6,7,8,9,10,11,12,13,14,15,16,17,18,19,20,21,22,23,24,25,26..., dimensions={0} | all-to-all | bytes 262144 | tf_op jit(solution)/shard_map/all_to_all | solution.py:345
  22.4 12.6 %all_to_all.41 = bf16[32,16,128]{2,1,0:T(8,128)(2,1)S(1)} all-to-all(bf16[32,16,128]{2,1,0:T(8,128)(2,1)S(1)} %bitcast.29), channel_id=1, replica_groups={{0,1,2,3,4,5,6,7,8,9,10,11,12,13,14,15,16,17,18,19,20,21,22,23,24,25,26..., dimensions={0} | all-to-all | bytes 262144 | tf_op jit(solution)/shard_map/all_to_all | solution.py:345
  35.0 0.2 shard_map.69
  35.3 21.3 %all_to_all.42 = f32[16,1,1024]{2,1,0:T(1,128)S(1)} all-to-all(f32[16,1,1024]{2,1,0:T(1,128)S(1)} %bitcast.35), channel_id=1, replica_groups={{0,32,64,96,128,160,192,224,256,288,320,352,384,416,448,480},{1,33,65,9..., dimensions={0} | all-to-all | bytes 131072 | tf_op jit(solution)/shard_map/all_to_all | solution.py:345
  56.5 10.4 %all_to_all.43 = f32[16,1,1024]{2,1,0:T(1,128)S(1)} all-to-all(f32[16,1,1024]{2,1,0:T(1,128)S(1)} %bitcast.34), channel_id=1, replica_groups={{0,32,64,96,128,160,192,224,256,288,320,352,384,416,448,480},{1,33,65,9..., dimensions={0} | all-to-all | bytes 131072 | tf_op jit(solution)/shard_map/all_to_all | solution.py:345
  66.9 0.5 shard_map.71
  67.5 0.0 copy-start
  67.5 15.2 %all_to_all.44 = f32[32,1,2176]{2,1,0:T(1,128)S(1)} all-to-all(f32[32,1,2176]{2,1,0:T(1,128)S(1)} %bitcast.31), channel_id=1, replica_groups={{0,1,2,3,4,5,6,7,8,9,10,11,12,13,14,15,16,17,18,19,20,21,22,23,24,25,26..., dimensions={0} | all-to-all | bytes 557056 | tf_op jit(solution)/shard_map/all_to_all | solution.py:345
  82.7 0.1 shard_map.72
  82.8 0.0 copy-start.1
  82.8 15.0 %all_to_all.45 = f32[32,1,2176]{2,1,0:T(1,128)S(1)} all-to-all(f32[32,1,2176]{2,1,0:T(1,128)S(1)} %bitcast.27), channel_id=1, replica_groups={{0,1,2,3,4,5,6,7,8,9,10,11,12,13,14,15,16,17,18,19,20,21,22,23,24,25,26..., dimensions={0} | all-to-all | bytes 557056 | tf_op jit(solution)/shard_map/all_to_all | solution.py:345
  97.8 2.7 %shard_map.73 = (f32[512,128]{1,0:T(8,128)S(1)}, f32[64,256]{1,0:T(8,128)S(1)}, bf16[16,24,128]{2,1,0:T(8,128)(2,1)S(1)}) custom-call(f32[544,128]{1,0:T(8,128)S(1)} %bitcast.25, f32[64,256]{1,0:T(8,128)S(1)} %get-tuple-element.16.krylov), custom_call_target="tpu_custom_call" | custom-call | tf_op jit(solution)/shard_map/pallas_call | solution.py:381
  100.5 14.4 %all_to_all.46.grams = bf16[16,24,128]{2,1,0:T(8,128)(2,1)S(1)} all-to-all(bf16[16,24,128]{2,1,0:T(8,128)(2,1)S(1)} %get-tuple-element.17), channel_id=1, replica_groups={{0,32,64,96,128,160,192,224,256,288,320,352,384,416,448,480},{1,33,65,9..., dimensions={0} | all-to-all | bytes 196608 | tf_op jit(solution)/shard_map/all_to_all | solution.py:345
  114.9 0.0 copy-done
  114.9 0.0 copy-done.1
  114.9 4.1 %shard_map.74 = (f32[2,512,256]{2,1,0:T(8,128)}, f32[2,512,256]{2,1,0:T(8,128)}, f32[64,128]{1,0:T(8,128)S(1)}) custom-call(bf16[16,24,128]{2,1,0:T(8,128)(2,1)S(1)} %all_to_all.46.grams, f32[64,256]{1,0:T(8,128)S(1)} %get-tuple-element.18.subspace, bf16[2,512,256]{2,1,0:T(8,128)(2,1)S(1)} %bitcast.24, f32[2,512,256]{2,1,0:T(8,128)S(1)} %bitcast.22, ...), custom_call_target="tpu_custom_call" | custom-call | tf_op jit(solution)/shard_map/pallas_call | solution.py:389
  119.0 9.8 %all_to_all.47 = f32[16,1,512]{2,1,0:T(1,128)S(1)} all-to-all(f32[16,1,512]{2,1,0:T(1,128)S(1)} %bitcast.38), channel_id=1, replica_groups={{0,32,64,96,128,160,192,224,256,288,320,352,384,416,448,480},{1,33,65,9..., dimensions={0} | all-to-all | bytes 65536 | tf_op jit(solution)/shard_map/all_to_all | solution.py:345
  128.8 0.6 shard_map.75
  (2 shorter events, 0.1 us)
Async XLA Ops:
  67.5 47.4 %copy-start = (f32[1024,256]{1,0:T(8,128)S(1)}, f32[1024,256]{1,0:T(8,128)}, u32[]{:S(2)}) copy-start(f32[1024,256]{1,0:T(8,128)} %param.6) | copy-start | bytes 3145732
  82.8 32.1 %copy-start.1 = (bf16[1024,256]{1,0:T(8,128)(2,1)S(1)}, bf16[1024,256]{1,0:T(8,128)(2,1)}, u32[]{:S(2)}) copy-start(bf16[1024,256]{1,0:T(8,128)(2,1)} %param.4) | copy-start | bytes 1572868
